TPU v7x, 128 devices: a whole 4x4x4 slice. The times are simulated.
128 devices in a mesh: dp: 4 (over z_hi, core), seq: 32 (over x, z_lo, y).
Axes of the slice: x: 4, y: 4, z: 4 (z_hi: 2, z_lo: 2; z = z_hi * 2 + z_lo), core: 2. Of those that a mesh axis runs over, the one named last changes fastest.
Arguments:
- frames_in: bfloat16 [384, 256, 1152], P(('dp', 'seq')), parts along dimension 0, may hold values from -18 to 18
- modulation: float32 [12, 1152], P('dp'), parts along dimension 0, may hold values from -3 to 3
- caption_kv: bfloat16 [480, 2304], P('dp', 'seq'), parts along dimension 0, may hold values from -18 to 18
- caption_len: int32 [4], P('dp'), parts along dimension 0, may hold values from 30 to 120
- w_spatial_qkv: bfloat16 [1152, 3456], replicated, may hold values from -0.1875 to 0.1875
- w_spatial_proj: bfloat16 [1152, 1152], replicated, may hold values from -0.1875 to 0.1875
- w_temporal_qkv: bfloat16 [1152, 3456], replicated, may hold values from -0.1875 to 0.1875
- w_temporal_proj: bfloat16 [1152, 1152], replicated, may hold values from -0.1875 to 0.1875
- w_cross_q: bfloat16 [1152, 1152], P('seq'), may hold values from -0.1875 to 0.1875
- w_cross_out: bfloat16 [1152, 1152], P('seq'), may hold values from -0.1875 to 0.1875
Outputs:
- block_out: bfloat16 [384, 256, 1152], P(('dp', 'seq')), parts along dimension 0
There are 4 independent parts, one for each index of `dp`. A program takes and returns all parts, laid end to end along the dimension named above; an argument that names none is the same for every part. Nothing has to cross between parts.
Inputs may be any that keep to these rules, and one draw needn't show every extreme that they name: At least a quarter of the 120 caption slots are valid; slots from caption_len on are padding.
All inputs are finite; a program needn't handle non-finite values.
Results may differ from a plain program's by a relative error of at most 0.034.
Values may be sent and summed in bfloat16 or wider, within the bound.
A program may use at most 128 MiB of HBM per device.

v0:
```python
import jax
import jax.numpy as jnp
from jax import lax
from jax.sharding import PartitionSpec as P

HEADS = 16
HEAD = 72


def layer_normed(inputs):
    widened = inputs.astype(jnp.float32)
    centered = widened - jnp.mean(widened, axis=-1, keepdims=True)
    variance = jnp.mean(centered * centered, axis=-1, keepdims=True)
    return centered * lax.rsqrt(variance + 1e-06)


def softmax_bf16(scores):
    maximum = jnp.max(scores, axis=-1, keepdims=True)
    exponent = jnp.exp(scores - maximum)
    return (exponent / jnp.sum(exponent, axis=-1, keepdims=True)).astype(jnp.bfloat16)


def split_heads(inputs):
    return inputs.reshape(inputs.shape[:-1] + (HEADS, HEAD))


def project(inputs, weight):
    flat = inputs.reshape(-1, inputs.shape[-1])
    product = jnp.dot(flat, weight, preferred_element_type=jnp.float32)
    return product.reshape(inputs.shape[:-1] + (weight.shape[1],))


def frame_attend(queries, key_rows, value_rows):
    scores = jnp.einsum(
        "fqhe,fkhe->fhqk",
        split_heads(queries),
        split_heads(key_rows),
        preferred_element_type=jnp.float32,
    ) * HEAD ** (-0.5)
    weights = softmax_bf16(scores)
    mixture = jnp.einsum(
        "fhqk,fkhe->fqhe", weights, split_heads(value_rows), preferred_element_type=jnp.float32
    )
    return mixture.astype(jnp.bfloat16).reshape(queries.shape)


def patch_attend(queries, key_rows, value_rows):
    scores = jnp.einsum(
        "qphe,kphe->phqk",
        split_heads(queries),
        split_heads(key_rows),
        preferred_element_type=jnp.float32,
    ) * HEAD ** (-0.5)
    weights = softmax_bf16(scores)
    mixture = jnp.einsum(
        "phqk,kphe->qphe", weights, split_heads(value_rows), preferred_element_type=jnp.float32
    )
    return mixture.astype(jnp.bfloat16).reshape(queries.shape)


def caption_attend(queries, key_rows, value_rows, allowed):
    scores = jnp.einsum(
        "qhe,khe->hqk",
        split_heads(queries),
        split_heads(key_rows),
        preferred_element_type=jnp.float32,
    ) * HEAD ** (-0.5)
    scores = jnp.where(allowed[None, None, :], scores, -jnp.inf)
    weights = softmax_bf16(scores)
    mixture = jnp.einsum(
        "hqk,khe->qhe", weights, split_heads(value_rows), preferred_element_type=jnp.float32
    )
    return mixture.astype(jnp.bfloat16).reshape(queries.shape)


def shards(
    frames_in,
    modulation,
    caption_kv,
    caption_len,
    w_spatial_qkv,
    w_spatial_proj,
    w_temporal_qkv,
    w_temporal_proj,
    w_cross_q,
    w_cross_out,
):
    model_width = frames_in.shape[-1]
    frame_count = frames_in.shape[0]
    seq_count = lax.axis_size("seq")
    local_patches = frames_in.shape[1] // seq_count
    offset_row = modulation[0]
    scale_row = modulation[1]
    gate_row = modulation[2]
    modulated = (layer_normed(frames_in) * (1.0 + scale_row) + offset_row).astype(jnp.bfloat16)
    spatial_qkv = project(modulated, w_spatial_qkv).astype(jnp.bfloat16)
    spatial_mix = frame_attend(
        spatial_qkv[..., :model_width],
        spatial_qkv[..., model_width : 2 * model_width],
        spatial_qkv[..., 2 * model_width :],
    )
    after_spatial = (
        frames_in.astype(jnp.float32) + gate_row * project(spatial_mix, w_spatial_proj)
    ).astype(jnp.bfloat16)
    caption = lax.all_gather(caption_kv, "seq", axis=1, tiled=True)
    caption_keys = caption[:, :model_width]
    caption_values = caption[:, model_width:]
    allowed = jnp.arange(caption.shape[0], dtype=jnp.int32) < caption_len[0]
    temporal_qkv = project(after_spatial, w_temporal_qkv).astype(jnp.bfloat16)
    slotted = temporal_qkv.reshape(frame_count, seq_count, local_patches, 3 * model_width)
    qkv_block = lax.all_to_all(slotted, "seq", split_axis=1, concat_axis=0, tiled=True)
    flat = qkv_block.reshape(qkv_block.shape[0], -1, qkv_block.shape[-1])
    mixed = patch_attend(
        flat[..., :model_width],
        flat[..., model_width : 2 * model_width],
        flat[..., 2 * model_width :],
    )
    mixture_patch = mixed.reshape(qkv_block.shape[:-1] + (model_width,))
    mixture_frames = lax.all_to_all(
        mixture_patch, "seq", split_axis=0, concat_axis=1, tiled=True
    ).reshape(frames_in.shape)
    after_temporal = (
        after_spatial.astype(jnp.float32) + gate_row * project(mixture_frames, w_temporal_proj)
    ).astype(jnp.bfloat16)
    token_rows = after_temporal.reshape(-1, model_width)
    columns = token_rows
    cross_query = jnp.dot(
        columns,
        lax.all_gather(w_cross_q, "seq", axis=0, tiled=True),
        preferred_element_type=jnp.float32,
    ).astype(jnp.bfloat16)
    caption_mix = caption_attend(cross_query, caption_keys, caption_values, allowed)
    columns = caption_mix
    branch = jnp.dot(
        columns,
        lax.all_gather(w_cross_out, "seq", axis=0, tiled=True),
        preferred_element_type=jnp.float32,
    )
    return (token_rows.astype(jnp.float32) + branch).astype(jnp.bfloat16).reshape(frames_in.shape)


def solution(mesh):
    in_specs = (
        P(("dp", "seq"), None, None),
        P("dp", None),
        P("dp", "seq"),
        P("dp"),
        P(),
        P(),
        P(),
        P(),
        P("seq", None),
        P("seq", None),
    )
    out_specs = P(("dp", "seq"), None, None)
    return jax.shard_map(shards, mesh=mesh, in_specs=in_specs, out_specs=out_specs, check_vma=False)
```

profile of v0, /device:TPU:0, one launch (start us, length us, event | category | flops | bytes accessed | tf_op | source)
XLA Modules:
  0.0 418.7 jit_solution(7739037683982893525)
XLA Ops:
  8.2 1.8 convert_reduce_fusion
  10.7 10.3 %fusion.10 = bf16[3,256,3456]{2,1,0:T(8,128)(2,1)S(1)} fusion(bf16[1152,3456]{1,0:T(8,128)(2,1)} %param.14, bf16[3,256,1152]{2,1,0:T(8,128)(2,1)S(1)} %copy-done.2, f32[1152]{0:T(1024)S(1)} %get-tuple-element.6, f32[1152]{0:T(1024)S(1)} %get-tuple-element.7, f32[3,256]{1,0:T(4,128)S(1)} %add_rsqrt_fusion, f32[3,256]{1,0:T(4,128)S(1)} %broadcast_multiply_fusion), kind=kOutput, calls=%fused_computation.11 | convolution fusion | flops 6123257856 | bytes 15055872 | tf_op jit(solution)/shard_map/dot_general | solution.py:29
  21.0 2.5 fusion.64
  23.5 3.8 copy.33
  27.3 3.8 copy.34
  31.2 3.8 copy.32
  35.0 10.8 %fusion.66 = (f32[3,16,256]{2,1,0:T(8,128)S(1)}, f32[3,16,256,256]{2,3,1,0:T(8,128)}) fusion(bf16[3,256,16,72]{1,3,2,0:T(8,128)(2,1)} %bitcast.80, bf16[3,256,16,72]{1,3,2,0:T(8,128)(2,1)} %bitcast.81), kind=kOutput, calls=%fused_computation.74 | convolution fusion | flops 462422272 | bytes 16171008 | tf_op jit(solution)/shard_map/sub | solution.py:19
  45.8 6.5 %fusion.52 = bf16[3,16,72,256]{3,2,1,0:T(8,128)(2,1)S(1)} fusion(bf16[3,256,16,72]{1,3,2,0:T(8,128)(2,1)} %bitcast.82, f32[3,16,256,256]{2,3,1,0:T(8,128)} %get-tuple-element.17, f32[3,16,256]{2,1,0:T(8,128)S(1)} %get-tuple-element.16), kind=kOutput, calls=%fused_computation.57 | convolution fusion | flops 460161024 | bytes 16171008 | tf_op jit(solution)/shard_map/fhqk,fkhe->fqhe/dot_general | solution.py:41
  52.3 2.8 fusion.34
  56.3 9.7 %fusion.18 = bf16[3,32,8,3456]{3,2,1,0:T(8,128)(2,1)S(1)} fusion(bf16[3,256,1152]{2,1,0:T(8,128)(2,1)S(1)} %fusion.34, bf16[1152,3456]{1,0:T(8,128)(2,1)} %param.16), kind=kOutput, calls=%fused_computation.17 | convolution fusion | flops 6117949440 | bytes 15040512 | tf_op jit(solution)/shard_map/dot_general | solution.py:29
  66.1 2.7 copy.37
  68.8 8.9 %all-to-all-start = ((bf16[3,32,8,3456]{3,2,0,1:T(8,128)(2,1)}), bf16[3,32,8,3456]{3,2,0,1:T(8,128)(2,1)}, u32[]{:S(2)}, u32[]{:S(2)}) async-start(bf16[3,32,8,3456]{3,2,0,1:T(8,128)(2,1)} %copy.37), calls=%async_computation | async-start | bytes 10616832 | tf_op jit(solution)/shard_map/all_to_all | solution.py:111
  78.4 80.9 %all-to-all-done = bf16[3,32,8,3456]{3,2,0,1:T(8,128)(2,1)} async-done(((bf16[3,32,8,3456]{3,2,0,1:T(8,128)(2,1)}), bf16[3,32,8,3456]{3,2,0,1:T(8,128)(2,1)}, u32[]{:S(2)}, u32[]{:S(2)}) %all-to-all-start) | async-done | bytes 5308448 | tf_op jit(solution)/shard_map/all_to_all | solution.py:111
  159.3 4.8 %fusion.63 = (bf16[96,8,1152]{2,1,0:T(8,128)(2,1)}, bf16[96,8,1152]{2,1,0:T(8,128)(2,1)}, bf16[96,8,1152]{2,1,0:T(8,128)(2,1)S(1)}) fusion(bf16[96,8,3456]{2,1,0:T(8,128)(2,1)} %bitcast.11), kind=kLoop, calls=%fused_computation.71 | loop fusion | bytes 10616832 | tf_op jit(solution)/shard_map/slice | solution.py:115
  164.1 4.1 copy.39
  168.2 4.2 copy.40
  172.4 2.6 copy.38
  175.0 7.8 %fusion.67 = (f32[8,16,96]{2,1,0:T(8,128)S(1)}, f32[8,16,96,96]{2,3,1,0:T(8,128)}) fusion(bf16[96,8,16,72]{0,3,2,1:T(8,128)(2,1)} %bitcast.76, bf16[96,8,16,72]{0,3,2,1:T(8,128)(2,1)} %bitcast.77), kind=kOutput, calls=%fused_computation.75 | convolution fusion | flops 173408352 | bytes 8306688 | tf_op jit(solution)/shard_map/sub | solution.py:19
  182.8 5.6 %fusion.43 = bf16[8,16,72,96]{3,2,1,0:T(8,128)(2,1)} fusion(bf16[96,8,16,72]{0,3,2,1:T(8,128)(2,1)S(1)} %bitcast.78, f32[8,16,96,96]{2,3,1,0:T(8,128)} %get-tuple-element.19, f32[8,16,96]{2,1,0:T(8,128)S(1)} %get-tuple-element.18), kind=kOutput, calls=%fused_computation.49 | convolution fusion | flops 173113344 | bytes 8306688 | tf_op jit(solution)/shard_map/phqk,kphe->qphe/dot_general | solution.py:55
  188.4 4.3 %copy.42 = bf16[96,1,8,1152]{3,2,1,0:T(8,128)(2,1)} copy(bf16[96,1,8,1152]{0,3,2,1:T(8,128)(2,1)} %bitcast.79) | data formatting | bytes 3538944 | tf_op jit(solution)/shard_map/reshape;reshape | solution.py:118
  192.7 8.2 %all-to-all-start.1 = ((bf16[96,1,8,1152]{3,2,1,0:T(8,128)(2,1)}), bf16[96,1,8,1152]{3,2,1,0:T(8,128)(2,1)}, u32[]{:S(2)}, u32[]{:S(2)}) async-start(bf16[96,1,8,1152]{3,2,1,0:T(8,128)(2,1)} %copy.42), calls=%async_computation.1 | async-start | bytes 3538944 | tf_op jit(solution)/shard_map/all_to_all | solution.py:119
  201.5 96.0 %all_gather.10 = bf16[120,2304]{0,1:T(8,128)(2,1)S(1)} all-gather(bf16[120,72]{0,1:T(8,128)(2,1)S(1)} %copy-done.6), channel_id=1, replica_groups=mesh['dp'=4,'seq'=32] {'seq'}, dimensions={1}, use_global_device_ids=true | all-gather | bytes 570240 | tf_op jit(solution)/shard_map/all_gather | solution.py:105
  297.6 3.8 reshape.104
  301.5 79.4 %all-gather.7.cloned.1.call-done = bf16[32,36,1152]{2,1,0:T(8,128)(2,1)} async-done(((bf16[1,36,1152]{2,1,0:T(8,128)(2,1)}), bf16[32,36,1152]{2,1,0:T(8,128)(2,1)}) %all-gather.7.cloned.1.call-update) | async-done | bytes 2654224 | tf_op jit(solution)/shard_map/all_gather | solution.py:136
  380.8 5.2 %reshape.106 = bf16[1152,1152]{1,0:T(8,128)(2,1)} reshape(bf16[32,36,1152]{2,1,0:T(8,128)(2,1)} %all-gather.7.cloned.1.call-done) | data formatting | bytes 5308416
  386.0 5.5 %fusion.33 = bf16[3,256,1152]{2,1,0:T(8,128)(2,1)S(1)} fusion(bf16[3,256,1152]{2,1,0:T(8,128)(2,1)} %copy-done.9, bf16[1152,1152]{1,0:T(8,128)(2,1)} %param.17, bf16[3,32,1,8,1152]{4,3,0,1,2:T(8,128)(2,1)} %bitcast.20, f32[1152]{0:T(1024)S(1)} %get-tuple-element.5), kind=kOutput, calls=%fused_computation.38 | convolution fusion | flops 2041970688 | bytes 7967232 | tf_op jit(solution)/shard_map/dot_general | solution.py:29
  391.5 1.3 copy-done.7
  392.8 3.8 convolution_convert_fusion
  396.6 2.6 copy.44
  399.2 4.9 %fusion.68 = (f32[16,768]{1,0:T(8,128)S(1)}, f32[16,768,120]{1,2,0:T(8,128)}) fusion(pred[120]{0:T(512)(128)(4,1)S(1)} %iota_compare_fusion, bf16[768,16,72]{0,2,1:T(8,128)(2,1)S(1)} %bitcast.83, bf16[120,16,72]{0,2,1:T(8,128)(2,1)S(1)} %bitcast.85), kind=kOutput, calls=%fused_computation.76 | convolution fusion | flops 218234992 | bytes 7993464 | tf_op jit(solution)/shard_map/sub | solution.py:19
  404.1 3.5 fusion.51
  408.1 3.8 fusion.32
  (31 shorter events, 4.8 us)
Async XLA Ops:
  6.5 45.8 %copy-start = (bf16[1152,1152]{1,0:T(8,128)(2,1)S(1)}, bf16[1152,1152]{1,0:T(8,128)(2,1)}, u32[]{:S(2)}) copy-start(bf16[1152,1152]{1,0:T(8,128)(2,1)} %param.15) | copy-start | bytes 7962628
  6.5 291.1 %all-gather.5.cloned.1.call-start = ((), (), s32[]{:S(2)}) async-start(), calls=%async_computation.2 | async-start | bytes 3041280 | tf_op jit(solution)/shard_map/all_gather | solution.py:129
  7.3 2.8 copy-start.2
  45.8 6.5 %copy-start.3 = (bf16[3,256,1152]{2,1,0:T(8,128)(2,1)S(1)}, bf16[3,256,1152]{2,1,0:T(8,128)(2,1)}, u32[]{:S(2)}) copy-start(bf16[3,256,1152]{2,1,0:T(8,128)(2,1)} %param.10) | copy-start | bytes 5308420
  55.1 1.2 copy-start.9
  68.8 90.5 %all-to-all-start = ((bf16[3,32,8,3456]{3,2,0,1:T(8,128)(2,1)}), bf16[3,32,8,3456]{3,2,0,1:T(8,128)(2,1)}, u32[]{:S(2)}, u32[]{:S(2)}) async-start(bf16[3,32,8,3456]{3,2,0,1:T(8,128)(2,1)} %copy.37), calls=%async_computation | async-start | bytes 10616832 | tf_op jit(solution)/shard_map/all_to_all | solution.py:111
  77.7 303.2 %all-gather.7.cloned.1.call-start = ((), (), s32[]{:S(2)}) async-start(), calls=%async_computation.3 | async-start | bytes 3041280 | tf_op jit(solution)/shard_map/all_gather | solution.py:136
  175.0 7.8 %copy-start.5 = (bf16[96,8,1152]{0,2,1:T(8,128)(2,1)S(1)}, bf16[96,8,1152]{0,2,1:T(8,128)(2,1)}, u32[]{:S(2)}) copy-start(bf16[96,8,1152]{0,2,1:T(8,128)(2,1)} %copy.38) | copy-start | bytes 5308420
  192.7 8.8 %copy-start.6 = (bf16[120,72]{0,1:T(8,128)(2,1)S(1)}, bf16[120,72]{0,1:T(8,128)(2,1)}, u32[]{:S(2)}) copy-start(bf16[120,72]{0,1:T(8,128)(2,1)} %param.12) | copy-start | bytes 51844
  192.7 193.3 %all-to-all-start.1 = ((bf16[96,1,8,1152]{3,2,1,0:T(8,128)(2,1)}), bf16[96,1,8,1152]{3,2,1,0:T(8,128)(2,1)}, u32[]{:S(2)}, u32[]{:S(2)}) async-start(bf16[96,1,8,1152]{3,2,1,0:T(8,128)(2,1)} %copy.42), calls=%async_computation.1 | async-start | bytes 3538944 | tf_op jit(solution)/shard_map/all_to_all | solution.py:119
  391.5 1.3 copy-start.7
  404.1 3.5 copy-start.4
  404.1 4.0 copy-start.8
  408.1 3.8 copy-start.1
Sparse Core Ops, SparseCore 0:
  9.0 213.6 all-gather.4
  224.4 156.4 all-gather.6
where the time goes:
time: 420 us; the launch traced here: 419 us
  waiting for transfers between devices  162 us (39%)
  blocking collectives  96 us (23%)
  matrix products  74.9 us (18%)
  local copies, waits for them, and re-layouts  51.4 us (12%)
  starting transfers between devices  17.1 us (4%)
  between operations  14.2 us (3%)
    all_gather x1, blocking collectives, shards(): caption = lax.all_gather(caption_kv, 'seq', axis=1, tiled=True)  96 us
    all_to_all x1, waiting for transfers between devices, shards(): lax.all_to_all(slotted, 'seq', split_axis=1, concat_axis=0, tiled=True)  80.9 us
    all_gather x1, waiting for transfers between devices, shards(): lax.all_gather(w_cross_out, 'seq', axis=0, tiled=True)  79.4 us
    dot_general x4, matrix products, project(): product = jnp.dot(flat, weight, preferred_element_type=jnp.float32)  28.3 us
    sub x3, matrix products, softmax_bf16(): exponent = jnp.exp(scores - maximum)  23.4 us
    unnamed x22, local copies, waits for them, and re-layouts  12 us
    slice x2, local copies, waits for them, and re-layouts, shards(): flat[..., model_width:2 * model_width]  8.96 us
    all_to_all x1, starting transfers between devices, shards(): lax.all_to_all(slotted, 'seq', split_axis=1, concat_axis=0, tiled=True)  8.87 us
  transfers between devices with their start and end apart: 4, of which 2 were waited for; matrix products, arithmetic and copies ran while one was open for 25% of the time, Pallas kernels for 0%

commit v1 on v0

v1 whole, which is shorter than its diff:
```python
import functools
import math

import jax
import jax.numpy as jnp
from jax import lax
from jax.experimental import pallas as pl
from jax.experimental.pallas import tpu as pltpu
from jax.sharding import PartitionSpec as P

HEADS = 16
HEAD = 72
D = 1152
LANES = 128
SPAN = 128
SEQ = 32
LOCAL = 3
PATCH = 8
CAP = 120
ROWS = 256
BF = jnp.bfloat16
F32 = jnp.float32
MESH = pl.DeviceIdType.MESH
EXP_SCALE = HEAD ** (-0.5) * math.log2(math.e)
COLS = 384


def window(head):
    low = HEAD * head
    return low // LANES * LANES, -(-(low + HEAD) // LANES) * LANES


def dot_nt(a, b):
    return lax.dot_general(a, b, (((1,), (1,)), ((), ())), preferred_element_type=F32)


def dot_nn(a, b):
    return jnp.dot(a, b, preferred_element_type=F32)


def head_mask(head):
    first, last = window(head)
    lane = lax.broadcasted_iota(jnp.int32, (1, last - first), 1) + first
    return jnp.where((lane >= HEAD * head) & (lane < HEAD * (head + 1)), 1.0, 0.0).astype(BF)


def placed(head):
    first, last = window(head)
    shape = (LANES, last - first)
    feature = lax.broadcasted_iota(jnp.int32, shape, 0)
    lane = lax.broadcasted_iota(jnp.int32, shape, 1) + first
    return jnp.where((lane == feature + HEAD * head) & (feature < HEAD), 1.0, 0.0).astype(BF)


def frame_to_patch():
    row = lax.broadcasted_iota(jnp.int32, (ROWS, ROWS), 0)
    column = lax.broadcasted_iota(jnp.int32, (ROWS, ROWS), 1)
    return jnp.where(column == (row % SEQ) * PATCH + row // SEQ, 1.0, 0.0).astype(BF)


def patch_to_frame():
    row = lax.broadcasted_iota(jnp.int32, (ROWS, ROWS), 0)
    column = lax.broadcasted_iota(jnp.int32, (ROWS, ROWS), 1)
    return jnp.where(column == (row % PATCH) * SEQ + row // PATCH, 1.0, 0.0).astype(BF)


def attend_t(queries, keys, values_t):
    scores = dot_nt(keys, queries)
    top = jnp.max(scores, axis=0, keepdims=True)
    weights = jnp.exp2((scores - top) * EXP_SCALE)
    total = jnp.sum(weights, axis=0, keepdims=True)
    return dot_nn(values_t, weights.astype(BF)) * (1.0 / total)


def kernel(
    caption_len, frames_ref, modulation, caption_ref, wsqkv_ref, wsp_ref, wtqkv_ref, wtp_ref, wc_ref,
    out_ref,
    frames, wsqkv, wsp, wtqkv, wtp, wy, wg, cap, cap_scores, cap_values,
    modulated, qk, vt, mix_t, mix, sent, received, x, tqk, tv, tvt, tmix_t, tmix, weights_n,
    load_sem, y_send, y_recv, g_send, g_recv, s_send, s_recv, c_send, c_recv, f_send, f_recv, r_send, r_recv, local_sem,
):
    me = lax.axis_index("seq")
    dp = lax.axis_index("dp")
    core = dp % 2
    my_y = me % 4
    my_block = me // 4

    def peer_of(k):
        y = (me % 4 + k % 4) % 4
        x_ = (me // 8 + (k // 4) % 4) % 4
        z = (me // 4 + k // 16) % 2
        return x_ * 8 + z * 4 + y

    barrier = pltpu.get_barrier_semaphore()

    @pl.loop(1, SEQ)
    def _(k):
        pl.semaphore_signal(barrier, inc=1, device_id={"seq": peer_of(k)}, device_id_type=MESH)

    pl.semaphore_signal(barrier, inc=1, device_id={"dp": dp + 1 - 2 * core}, device_id_type=MESH)

    loads = [
        pltpu.make_async_copy(frames_ref, frames, load_sem.at[0]),
        pltpu.make_async_copy(wsqkv_ref.at[:, :D], wsqkv.at[:, :D], load_sem.at[1]),
        pltpu.make_async_copy(wsqkv_ref.at[:, D : 2 * D], wsqkv.at[:, D : 2 * D], load_sem.at[2]),
        pltpu.make_async_copy(wsqkv_ref.at[:, 2 * D :], wsqkv.at[:, 2 * D :], load_sem.at[3]),
        pltpu.make_async_copy(wsp_ref, wsp, load_sem.at[4]),
        pltpu.make_async_copy(wtqkv_ref, wtqkv, load_sem.at[5]),
        pltpu.make_async_copy(wtp_ref, wtp, load_sem.at[6]),
    ]
    for load in loads:
        load.start()
    own_caption = pltpu.make_async_copy(caption_ref, cap.at[me], local_sem.at[0])
    own_caption.start()
    own_weight = pltpu.make_async_copy(wc_ref.at[core], wy.at[my_y], local_sem.at[1])
    own_weight.start()

    pl.semaphore_wait(barrier, SEQ)

    @pl.loop(1, 4)
    def _(k):
        y = (my_y + k) % 4
        pltpu.make_async_remote_copy(
            wc_ref.at[core], wy.at[my_y], y_send, y_recv, device_id={"seq": my_block * 4 + y}, device_id_type=MESH
        ).start()

    @pl.loop(1, SEQ)
    def _(k):
        pltpu.make_async_remote_copy(
            caption_ref, cap.at[me], c_send, c_recv, device_id={"seq": peer_of(k)}, device_id_type=MESH
        ).start()

    def block_peer(k):
        x_ = (me // 8 + k % 4) % 4
        z = (me // 4 + k // 4) % 2
        return x_ * 8 + z * 4 + my_y

    def gather_blocks():
        own_weight.wait()
        pltpu.make_async_copy(wy.at[pl.ds(0, 3)], wy.at[pl.ds(0, 3)], y_recv).wait()
        for c in range(0, D, COLS):
            total = None
            for y in range(4):
                row = lax.broadcasted_iota(jnp.int32, (144, 36), 0)
                column = lax.broadcasted_iota(jnp.int32, (144, 36), 1)
                place = jnp.where(row == column + 36 * y, 1.0, 0.0).astype(BF)
                term = dot_nn(place, wy[y, :, c : c + COLS])
                total = term if total is None else total + term
            wg[core, my_block, :, c : c + COLS] = total.astype(BF)

        @pl.loop(1, 8)
        def _(k):
            pltpu.make_async_remote_copy(
                wg.at[core, my_block], wg.at[core, my_block], g_send, g_recv,
                device_id={"seq": block_peer(k)}, device_id_type=MESH,
            ).start()

    def swap_copy():
        return pltpu.make_async_remote_copy(
            wg.at[core], wg.at[core], s_send, s_recv, device_id={"dp": dp + 1 - 2 * core}, device_id_type=MESH
        )

    def swap_weights():
        pltpu.make_async_copy(wg.at[core, pl.ds(0, 7)], wg.at[core, pl.ds(0, 7)], g_recv).wait()
        swap_copy().start()

    def spatial(f, _):
        @pl.when(f == 0)
        def _():
            loads[0].wait()

        @pl.loop(0, ROWS // 32)
        def _(r):
            rows = pl.ds(pl.multiple_of(r * 32, 32), 32)
            wide = frames[f, rows, :].astype(F32)
            centered = wide - jnp.mean(wide, axis=-1, keepdims=True)
            variance = jnp.mean(centered * centered, axis=-1, keepdims=True)
            normed = centered * lax.rsqrt(variance + 1e-06)
            modulated[rows, :] = (normed * (1.0 + modulation[1:2, :]) + modulation[0:1, :]).astype(BF)

        for part in range(3):
            @pl.when(f == 0)
            def _():
                loads[1 + part].wait()

            for c in range(0, D, COLS):
                product = dot_nn(modulated[...], wsqkv[:, part * D + c : part * D + c + COLS])
                if part < 2:
                    qk[:, part * D + c : part * D + c + COLS] = product.astype(BF)
                else:
                    vt[c : c + COLS, :] = product.T

        for head in range(HEADS):
            first, last = window(head)
            keys = qk[:, D + first : D + last] * head_mask(head)
            values_t = vt[HEAD * head : HEAD * (head + 1), :].astype(BF)
            mix_t[HEAD * head : HEAD * (head + 1), :] = attend_t(qk[:, first:last], keys, values_t)

        for c in range(0, D, COLS):
            mix[:, c : c + COLS] = mix_t[c : c + COLS, :].T.astype(BF)

        @pl.when(f == 0)
        def _():
            loads[4].wait()

        for c in range(0, D, COLS):
            branch = dot_nn(mix[...], wsp[:, c : c + COLS])
            after = frames[f, :, c : c + COLS].astype(F32) + modulation[2:3, c : c + COLS] * branch
            sent[f, :, :, c : c + COLS] = after.reshape(SEQ, PATCH, COLS).astype(BF)

        @pl.loop(1, SEQ)
        def _(k):
            peer = peer_of(k)
            pltpu.make_async_remote_copy(
                sent.at[f, peer], received.at[f, me], f_send.at[f], f_recv.at[f],
                device_id={"seq": peer}, device_id_type=MESH,
            ).start()

        received[f, me] = sent[f, me]

        @pl.when(f == 0)
        def _():
            gather_blocks()

        @pl.when(f == 1)
        def _():
            swap_weights()

        return 0

    lax.fori_loop(0, LOCAL, spatial, 0)

    def temporal_qkv(f, _):
        pltpu.make_async_copy(
            received.at[f, pl.ds(0, SEQ - 1)], received.at[f, pl.ds(0, SEQ - 1)], f_recv.at[f]
        ).wait()

        @pl.when(f == 0)
        def _():
            loads[5].wait()

        order = frame_to_patch()
        for c in range(0, D, COLS):
            block = received[f, :, :, c : c + COLS].astype(F32).reshape(ROWS, COLS).astype(BF)
            x[f, :, c : c + COLS] = dot_nn(order, block).astype(BF)
        frame_rows = pl.ds(pl.multiple_of(f * SEQ, SEQ), SEQ)
        for c in range(0, 3 * D, COLS):
            product = dot_nn(x[f], wtqkv[:, c : c + COLS]).astype(BF).reshape(PATCH, SEQ, COLS)
            if c < 2 * D:
                tqk[:, frame_rows, c : c + COLS] = product
            else:
                tv[:, frame_rows, c - 2 * D : c - 2 * D + COLS] = product
        return 0

    lax.fori_loop(0, LOCAL, temporal_qkv, 0)

    def temporal(p, _):
        frames_all = LOCAL * SEQ
        for c in range(0, D, COLS):
            tvt[c : c + COLS, :] = tv[p, :, c : c + COLS].astype(F32).T
        for head in range(HEADS):
            first, last = window(head)
            keys = tqk[p, :, D + first : D + last] * head_mask(head)
            values_t = tvt[HEAD * head : HEAD * (head + 1), :frames_all].astype(BF)
            tmix_t[HEAD * head : HEAD * (head + 1), :frames_all] = attend_t(tqk[p, :, first:last], keys, values_t)
        for c in range(0, D, COLS):
            block = tmix_t[c : c + COLS, :].T.astype(BF)
            for f in range(LOCAL):
                tmix[f, pl.ds(pl.multiple_of(p * SEQ, SEQ), SEQ), c : c + COLS] = block[f * SEQ : (f + 1) * SEQ]
        return 0

    tv[:, LOCAL * SEQ :, :] = jnp.zeros((PATCH, LANES - LOCAL * SEQ, D), BF)
    tmix_t[...] = jnp.zeros((D, LANES), F32)
    lax.fori_loop(0, PATCH, temporal, 0)

    own_caption.wait()
    pltpu.make_async_copy(cap.at[pl.ds(0, SEQ - 1)], cap.at[pl.ds(0, SEQ - 1)], c_recv).wait()
    swap_copy().wait()
    for head in range(HEADS):
        first, last = window(head)
        place = placed(head)
        keys = dot_nn(cap[head], place).astype(BF)
        values = dot_nn(cap[HEADS + head], place).astype(BF)
        cap_scores[head * SPAN : (head + 1) * SPAN, :] = dot_nt(
            keys, wg[0, :, :, first:last].reshape(D, last - first)
        ).astype(BF)
        rows = wg[1].reshape(D, D)[first:last]
        cap_values[head * SPAN : (head + 1) * SPAN, :] = dot_nn(values, rows).astype(BF)

    loads[6].wait()
    for f in range(LOCAL):
        pltpu.make_async_copy(
            sent.at[f, pl.ds(0, SEQ - 1)], sent.at[f, pl.ds(0, SEQ - 1)], f_send.at[f]
        ).wait()

    def finish(f, _):
        after = modulated
        for c in range(0, D, COLS):
            branch = dot_nn(tmix[f], wtp[:, c : c + COLS])
            after[:, c : c + COLS] = (
                x[f, :, c : c + COLS].astype(F32) + modulation[2:3, c : c + COLS] * branch
            ).astype(BF)
        allowed = lax.broadcasted_iota(jnp.int32, (SPAN, ROWS), 0) < caption_len[0]
        for head in range(HEADS):
            span = slice(head * SPAN, (head + 1) * SPAN)
            scores = jnp.where(allowed, dot_nt(cap_scores[span, :], after[...]), -1e30)
            top = jnp.max(scores, axis=0, keepdims=True)
            weights = jnp.exp2((scores - top) * EXP_SCALE)
            weights = weights * (1.0 / jnp.sum(weights, axis=0, keepdims=True))
            weights_n[:, span] = weights.T.astype(BF)
        order = patch_to_frame()
        for c in range(0, D, COLS):
            branch = dot_nn(weights_n[...], cap_values[:, c : c + COLS])
            rows = (after[:, c : c + COLS].astype(F32) + branch).astype(BF)
            sent[f, :, :, c : c + COLS] = dot_nn(order, rows).reshape(SEQ, PATCH, COLS).astype(BF)

        @pl.loop(1, SEQ)
        def _(k):
            peer = peer_of(k)
            pltpu.make_async_remote_copy(
                sent.at[f, peer], out_ref.at[f, me], r_send.at[f], r_recv.at[f],
                device_id={"seq": peer}, device_id_type=MESH,
            ).start()

        pltpu.make_async_copy(sent.at[f, me], out_ref.at[f, me], local_sem.at[2 + f]).start()
        return 0

    lax.fori_loop(0, LOCAL, finish, 0)

    for f in range(LOCAL):
        pltpu.make_async_copy(sent.at[f, me], out_ref.at[f, me], local_sem.at[2 + f]).wait()
        pltpu.make_async_copy(
            sent.at[f, pl.ds(0, SEQ - 1)], sent.at[f, pl.ds(0, SEQ - 1)], r_send.at[f]
        ).wait()
        pltpu.make_async_copy(
            out_ref.at[f, pl.ds(0, SEQ - 1)], out_ref.at[f, pl.ds(0, SEQ - 1)], r_recv.at[f]
        ).wait()
    pltpu.make_async_copy(wy.at[pl.ds(0, 3)], wy.at[pl.ds(0, 3)], y_send).wait()
    pltpu.make_async_copy(wg.at[core, pl.ds(0, 7)], wg.at[core, pl.ds(0, 7)], g_send).wait()
    pltpu.make_async_copy(cap.at[pl.ds(0, SEQ - 1)], cap.at[pl.ds(0, SEQ - 1)], c_send).wait()


def shards(
    frames_in, modulation, caption_kv, caption_len,
    w_spatial_qkv, w_spatial_proj, w_temporal_qkv, w_temporal_proj, w_cross_q, w_cross_out,
):
    caption = jnp.pad(caption_kv, ((0, SPAN - CAP), (0, LANES - HEAD)))
    crossed = jnp.stack([w_cross_q, w_cross_out])
    vmem = pl.BlockSpec(memory_space=pltpu.VMEM)
    whole = pl.BlockSpec(memory_space=pl.ANY)
    dma = pltpu.SemaphoreType.DMA
    out = pl.pallas_call(
        kernel,
        out_shape=jax.ShapeDtypeStruct((LOCAL, SEQ, PATCH, D), BF),
        in_specs=[pl.BlockSpec(memory_space=pltpu.SMEM), whole, vmem] + [whole] * 6,
        out_specs=whole,
        scratch_shapes=[
            pltpu.VMEM((LOCAL, ROWS, D), BF),
            pltpu.VMEM((D, 3 * D), BF),
            pltpu.VMEM((D, D), BF),
            pltpu.VMEM((D, 3 * D), BF),
            pltpu.VMEM((D, D), BF),
            pltpu.VMEM((4, 36, D), BF),
            pltpu.VMEM((2, 8, 144, D), BF),
            pltpu.VMEM((SEQ, SPAN, LANES), BF),
            pltpu.VMEM((HEADS * SPAN, D), BF),
            pltpu.VMEM((HEADS * SPAN, D), BF),
            pltpu.VMEM((ROWS, D), BF),
            pltpu.VMEM((ROWS, 2 * D), BF),
            pltpu.VMEM((D, ROWS), F32),
            pltpu.VMEM((D, ROWS), F32),
            pltpu.VMEM((ROWS, D), BF),
            pltpu.VMEM((LOCAL, SEQ, PATCH, D), BF),
            pltpu.VMEM((LOCAL, SEQ, PATCH, D), BF),
            pltpu.VMEM((LOCAL, ROWS, D), BF),
            pltpu.VMEM((PATCH, LOCAL * SEQ, 2 * D), BF),
            pltpu.VMEM((PATCH, LANES, D), BF),
            pltpu.VMEM((D, LANES), F32),
            pltpu.VMEM((D, LANES), F32),
            pltpu.VMEM((LOCAL, ROWS, D), BF),
            pltpu.VMEM((ROWS, HEADS * SPAN), BF),
            dma((7,)),
            dma, dma, dma, dma, dma, dma, dma, dma,
            dma((LOCAL,)), dma((LOCAL,)), dma((LOCAL,)), dma((LOCAL,)),
            dma((5,)),
        ],
        compiler_params=pltpu.CompilerParams(
            collective_id=0, has_side_effects=True, vmem_limit_bytes=65 * 1024 * 1024
        ),
        name="block",
    )(
        caption_len, frames_in, modulation, caption,
        w_spatial_qkv, w_spatial_proj, w_temporal_qkv, w_temporal_proj, crossed,
    )
    return out.reshape(frames_in.shape)


def solution(mesh):
    in_specs = (
        P(("dp", "seq"), None, None),
        P("dp", None),
        P("dp", "seq"),
        P("dp"),
        P(),
        P(),
        P(),
        P(),
        P("seq", None),
        P("seq", None),
    )
    out_specs = P(("dp", "seq"), None, None)
    return jax.shard_map(shards, mesh=mesh, in_specs=in_specs, out_specs=out_specs, check_vma=False)
```

time: 420 us -> 150 us (0.36)
  waiting for transfers between devices: 162 us -> 0 us
  Pallas kernels: 0 us -> 144 us
  blocking collectives: 96 us -> 0 us
  matrix products: 74.9 us -> 0 us
  local copies, waits for them, and re-layouts: 51.4 us -> 4.26 us
  starting transfers between devices: 17.1 us -> 0 us
  between operations: 14.2 us -> 0.67 us
    pallas_call x0 -> x1, Pallas kernels: none -> 144 us  [shards(): pl.pallas_call(kernel, out_shape=jax.ShapeDtypeStruct((LOCAL, SEQ, PATCH,...]
    all_gather x1 -> x0, blocking collectives: 96 us -> none  [shards(): caption = lax.all_gather(caption_kv, 'seq', axis=1, tiled=True)]
    all_to_all x2 -> x0, waiting for transfers between devices: 80.9 us -> none  [the longest x1 80.9 us: shards(): lax.all_to_all(slotted, 'seq', split_axis=1, concat_axis=0, tiled=True)]
    all_gather x2 -> x0, waiting for transfers between devices: 79.4 us -> none  [the longest x1 79.4 us: shards(): lax.all_gather(w_cross_out, 'seq', axis=0, tiled=True)]
    dot_general x9 -> x0, matrix products: 51.5 us -> none  [the longest x4 28.3 us: project(): product = jnp.dot(flat, weight, preferred_element_type=jnp.float32)]
    slice x9 -> x0, local copies, waits for them, and re-layouts: 29.8 us -> none  [the longest x2 8.96 us: shards(): flat[..., model_width:2 * model_width]]
    sub x3 -> x0, matrix products: 23.4 us -> none  [softmax_bf16(): exponent = jnp.exp(scores - maximum)]
    all_to_all x2 -> x0, starting transfers between devices: 17 us -> none  [the longest x1 8.87 us: shards(): lax.all_to_all(slotted, 'seq', split_axis=1, concat_axis=0, tiled=True)]
  transfers between devices with their start and end apart: 4 -> 0, of which waited for: 2 -> 0; matrix products, arithmetic and copies ran while one was open for 25% -> 0% of each run, Pallas kernels for 0% -> 0%
where the time goes in v1:
time: 150 us
  Pallas kernels  144 us (96%)
  local copies, waits for them, and re-layouts  4.26 us (3%)
  other arithmetic  1.63 us (1%)
    pallas_call x1, Pallas kernels, shards(): pl.pallas_call(kernel, out_shape=jax.ShapeDtypeStruct((LOCAL, SEQ, PATCH,...  144 us
    unnamed x2, local copies, waits for them, and re-layouts  3.64 us

profile of v1, /device:TPU:0, one launch (start us, length us, event | category | flops | bytes accessed | tf_op | source)
XLA Modules:
  0.0 150.2 jit_solution(5569520528828877855)
XLA Ops:
  0.7 0.8 copy.11
  1.5 0.6 pad.4.caption_ref
  2.1 1.6 %pad_maximum_fusion.wc_ref = bf16[2,36,1152]{2,1,0:T(8,128)(2,1)} fusion(bf16[1,36,1152]{2,1,0:T(8,128)(2,1)} %bitcast.4, bf16[1,36,1152]{2,1,0:T(8,128)(2,1)} %bitcast.5), kind=kLoop, calls=%fused_computation | loop fusion | flops 82944 | bytes 331776 | tf_op jit(solution)/shard_map/stack | solution.py:348
  3.7 143.6 %block.1 = bf16[3,32,8,1152]{3,2,1,0:T(8,128)(2,1)} custom-call(s32[1]{0:T(128)S(6)} %copy.13.caption_len, bf16[3,256,1152]{2,1,0:T(8,128)(2,1)} %frames_ref.1, f32[3,1152]{1,0:T(4,128)} %modulation.1, bf16[128,128]{1,0:T(8,128)(2,1)} %pad.4.caption_ref, bf16[1152,3456]{1,0:T(8,128)(2,1)} %wsqkv_ref.1, bf16[1152,1152]{1,0:T(8,128)(2,1)} %wsp_ref.1, ...), custom_call_target="tpu_custom_call" | custom-call | tf_op jit(solution)/shard_map/block/pallas_call | solution.py:352
  147.3 2.8 %copy.14 = bf16[3,256,1152]{2,1,0:T(8,128)(2,1)} copy(bf16[3,256,1152]{2,1,0:T(8,128)(2,1)} %bitcast.3) | data formatting | bytes 3538944

commit v2 on v1

v2 whole, which is shorter than its diff:
```python
import math

import jax
import jax.numpy as jnp
from jax import lax
from jax.experimental import pallas as pl
from jax.experimental.pallas import tpu as pltpu
from jax.sharding import PartitionSpec as P

HEADS = 16
HEAD = 72
D = 1152
LANES = 128
SEQ = 32
LOCAL = 3
PATCH = 8
CAP = 120
ROWS = 256
BF = jnp.bfloat16
F32 = jnp.float32
MESH = pl.DeviceIdType.MESH
EXP_SCALE = HEAD ** (-0.5) * math.log2(math.e)


def window(head):
    low = HEAD * head
    return low // LANES * LANES, -(-(low + HEAD) // LANES) * LANES


def dot_nt(a, b):
    return lax.dot_general(a, b, (((1,), (1,)), ((), ())), preferred_element_type=F32)


def dot_nn(a, b):
    return jnp.dot(a, b, preferred_element_type=F32)


def head_mask(head):
    first, last = window(head)
    lane = lax.broadcasted_iota(jnp.int32, (1, last - first), 1) + first
    return jnp.where((lane >= HEAD * head) & (lane < HEAD * (head + 1)), 1.0, 0.0).astype(BF)


def placed(head):
    first, last = window(head)
    shape = (HEAD, last - first)
    feature = lax.broadcasted_iota(jnp.int32, shape, 0)
    lane = lax.broadcasted_iota(jnp.int32, shape, 1) + first
    return jnp.where(lane == feature + HEAD * head, 1.0, 0.0).astype(BF)


def frame_to_patch():
    row = lax.broadcasted_iota(jnp.int32, (ROWS, ROWS), 0)
    column = lax.broadcasted_iota(jnp.int32, (ROWS, ROWS), 1)
    return jnp.where(column == (row % SEQ) * PATCH + row // SEQ, 1.0, 0.0).astype(BF)


def patch_to_frame():
    row = lax.broadcasted_iota(jnp.int32, (ROWS, ROWS), 0)
    column = lax.broadcasted_iota(jnp.int32, (ROWS, ROWS), 1)
    return jnp.where(column == (row % PATCH) * SEQ + row // PATCH, 1.0, 0.0).astype(BF)


def spans(first, last, step=512):
    return [(c, min(c + step, last)) for c in range(first, last, step)]


def attend_heads(score, value_t, store, buffers, group, allowed=None):
    scores, weights, inverse = buffers
    groups = HEADS // group

    def multiply(g):
        for i in range(group):
            scores[g % 2, i] = score(g * group + i)

    def soften(g):
        for i in range(group):
            rows = scores[g % 2, i]
            if allowed is not None:
                rows = jnp.where(allowed, rows, -1e30)
            top = jnp.max(rows, axis=0, keepdims=True)
            raised = jnp.exp2((rows - top) * EXP_SCALE)
            inverse[g % 2, i] = 1.0 / jnp.sum(raised, axis=0, keepdims=True)
            weights[g % 2, i] = raised.astype(BF)

    def mix(g):
        for i in range(group):
            store(g * group + i, dot_nn(value_t(g * group + i), weights[g % 2, i]) * inverse[g % 2, i])

    multiply(0)
    for g in range(groups):
        if g + 1 < groups:
            multiply(g + 1)
        soften(g)
        mix(g)


def landed(ref, semaphore):
    pltpu.make_async_copy(ref, ref, semaphore).wait()


def kernel(
    caption_len, frames_ref, modulation, caption_ref, wsqkv_ref, wsp_ref, wtqkv_ref, wtp_ref, wcq_ref, wco_ref,
    out_ref,
    frames, wsqkv, wsp, wtqkv, wtp, wy, wg, cap, cap_keys,
    modulated, qk, vt, mix_t, mix, sent, received, x, tqk, tv, tvt, tmix_t, tmix,
    scores, weights, inverse, tscores, tweights, tinverse, cscores, cweights, cinverse,
    load_sem, y_send, y_recv, g_send, g_recv, z_send, z_recv, s_send, s_recv, c_send, c_recv,
    f_send, f_recv, r_send, r_recv, local_sem,
):
    me = lax.axis_index("seq")
    dp = lax.axis_index("dp")
    core = dp % 2
    my_x, my_z, my_y = me // 8, (me // 4) % 2, me % 4
    other_core = dp + 1 - 2 * core
    across = (dp + 2) % 4

    def peer_of(k):
        y = (my_y + k % 4) % 4
        x_ = (my_x + (k // 4) % 4) % 4
        z = (my_z + k // 16) % 2
        return x_ * 8 + z * 4 + y

    facing = my_x * 8 + (1 - my_z) * 4 + my_y

    barrier = pltpu.get_barrier_semaphore()

    @pl.loop(1, SEQ)
    def _(k):
        pl.semaphore_signal(barrier, inc=1, device_id={"seq": peer_of(k)}, device_id_type=MESH)

    pl.semaphore_signal(barrier, inc=1, device_id={"dp": other_core}, device_id_type=MESH)
    pl.semaphore_signal(barrier, inc=1, device_id={"dp": across, "seq": facing}, device_id_type=MESH)

    def load(i):
        source, target = [
            (frames_ref.at[0], frames.at[0]),
            (wsqkv_ref.at[:, :1024], wsqkv.at[:, :1024]),
            (wsqkv_ref.at[:, 1024 : 2 * D], wsqkv.at[:, 1024 : 2 * D]),
            (wsqkv_ref.at[:, 2 * D :], wsqkv.at[:, 2 * D :]),
            (wsp_ref, wsp),
            (frames_ref.at[pl.ds(1, 2)], frames.at[pl.ds(1, 2)]),
            (wtqkv_ref, wtqkv),
            (wtp_ref, wtp),
        ][i]
        return pltpu.make_async_copy(source, target, load_sem.at[i])

    for i in range(3):
        load(i).start()
    own_caption = pltpu.make_async_copy(caption_ref, cap.at[me], local_sem.at[0])
    own_caption.start()

    def own_weight(source):
        return pltpu.make_async_copy(source, wy.at[my_x * 4 + my_y], local_sem.at[1])

    def first_gather(source):
        own_weight(source).start()

        @pl.loop(1, 4)
        def _(k):
            peer = (my_x + core * k) % 4 * 8 + my_z * 4 + (my_y + (1 - core) * k) % 4
            pltpu.make_async_remote_copy(
                source, wy.at[my_x * 4 + my_y], y_send, y_recv, device_id={"seq": peer}, device_id_type=MESH
            ).start()

    def second_gather():
        own_weight(wcq_ref).wait()
        landed(wy.at[pl.ds(0, 3)], y_recv)

        @pl.loop(0, 12)
        def _(n):
            k, i = 1 + n // 4, n % 4
            slot = (1 - core) * (my_x * 4 + i) + core * (i * 4 + my_y)
            peer = (my_x + (1 - core) * k) % 4 * 8 + my_z * 4 + (my_y + core * k) % 4
            pltpu.make_async_remote_copy(
                wy.at[slot], wy.at[slot], g_send, g_recv, device_id={"seq": peer}, device_id_type=MESH
            ).start()

    def third_gather():
        landed(wy.at[pl.ds(0, 12)], g_recv)
        for group in range(4):
            for first, last in spans(0, D):
                total = None
                for y in range(4):
                    row = lax.broadcasted_iota(jnp.int32, (144, 36), 0)
                    column = lax.broadcasted_iota(jnp.int32, (144, 36), 1)
                    place = jnp.where(row == column + 36 * y, 1.0, 0.0).astype(BF)
                    term = dot_nn(place, wy[group * 4 + y, :, first:last])
                    total = term if total is None else total + term
                wg[core, group * 2 + my_z, :, first:last] = total.astype(BF)
        for group in range(4):
            block = wg.at[core, group * 2 + my_z]
            pltpu.make_async_remote_copy(
                block, block, z_send, z_recv,
                device_id={"dp": dp if group == 0 else across, "seq": facing}, device_id_type=MESH,
            ).start()
            swap(group * 2 + my_z, 0).start()

    def swap(block, half):
        return pltpu.make_async_remote_copy(
            wg.at[core, block], wg.at[core, block], s_send.at[half], s_recv.at[half],
            device_id={"dp": other_core}, device_id_type=MESH,
        )

    def last_gather():
        landed(wg.at[core, pl.ds(0, 4)], z_recv)
        for group in range(4):
            swap(group * 2 + 1 - my_z, 1).start()

    def spatial(f, _):
        @pl.when(f == 0)
        def _():
            load(0).wait()

        @pl.when(f == 1)
        def _():
            load(5).wait()

        @pl.loop(0, ROWS // 32, unroll=4)
        def _(r):
            rows = pl.ds(pl.multiple_of(r * 32, 32), 32)
            wide = frames[f, rows, :].astype(F32)
            centered = wide - jnp.mean(wide, axis=-1, keepdims=True)
            variance = jnp.mean(centered * centered, axis=-1, keepdims=True)
            normed = centered * lax.rsqrt(variance + 1e-06)
            modulated[rows, :] = (normed * (1.0 + modulation[1:2, :]) + modulation[0:1, :]).astype(BF)

        @pl.when(f == 0)
        def _():
            pl.semaphore_wait(barrier, SEQ + 1)

            @pl.when(core == 0)
            def _():
                first_gather(wcq_ref)

            @pl.when(core == 1)
            def _():
                first_gather(wco_ref)

            load(1).wait()
            load(3).start()
            load(4).start()

        for first, last in spans(0, 1024):
            qk[:, first:last] = dot_nn(modulated[...], wsqkv[:, first:last]).astype(BF)

        @pl.when(f == 0)
        def _():
            load(2).wait()
            load(5).start()

        for first, last in spans(1024, 2 * D):
            qk[:, first:last] = dot_nn(modulated[...], wsqkv[:, first:last]).astype(BF)

        @pl.when(f == 0)
        def _():
            load(3).wait()
            load(6).start()
            second_gather()

            @pl.loop(1, SEQ)
            def _(k):
                pltpu.make_async_remote_copy(
                    caption_ref, cap.at[me], c_send, c_recv, device_id={"seq": peer_of(k)}, device_id_type=MESH
                ).start()

        for first, last in spans(0, D):
            vt[first:last, :] = dot_nn(modulated[...], wsqkv[:, 2 * D + first : 2 * D + last]).T

        @pl.when(f == 1)
        def _():
            third_gather()

        def score(head):
            first, last = window(head)
            return dot_nt(qk[:, D + first : D + last] * head_mask(head), qk[:, first:last])

        def store(head, rows):
            mix_t[HEAD * head : HEAD * (head + 1), :] = rows

        attend_heads(
            score, lambda head: vt[HEAD * head : HEAD * (head + 1), :].astype(BF), store, (scores, weights, inverse), 4
        )
        for first, last in spans(0, D):
            mix[:, first:last] = mix_t[first:last, :].T.astype(BF)

        @pl.when(f == 0)
        def _():
            load(4).wait()
            load(7).start()

        for first, last in spans(0, D):
            branch = dot_nn(mix[...], wsp[:, first:last])
            after = frames[f, :, first:last].astype(F32) + modulation[2:3, first:last] * branch
            sent[f, :, :, first:last] = after.reshape(SEQ, PATCH, last - first).astype(BF)

        @pl.loop(1, SEQ)
        def _(k):
            peer = peer_of(k)
            pltpu.make_async_remote_copy(
                sent.at[f, peer], received.at[f, me], f_send.at[f], f_recv.at[f],
                device_id={"seq": peer}, device_id_type=MESH,
            ).start()

        received[f, me] = sent[f, me]
        return 0

    lax.fori_loop(0, LOCAL, spatial, 0)

    def temporal_qkv(f, _):
        landed(received.at[f, pl.ds(0, SEQ - 1)], f_recv.at[f])

        @pl.when(f == 0)
        def _():
            load(6).wait()

        order = frame_to_patch()
        for first, last in spans(0, D):
            block = received[f, :, :, first:last].astype(F32).reshape(ROWS, last - first).astype(BF)
            x[f, :, first:last] = dot_nn(order, block).astype(BF)
        frame_rows = pl.ds(pl.multiple_of(f * SEQ, SEQ), SEQ)
        for first, last in spans(0, 2 * D):
            product = dot_nn(x[f], wtqkv[:, first:last]).astype(BF)
            tqk[:, frame_rows, first:last] = product.reshape(PATCH, SEQ, last - first)
        for first, last in spans(0, D):
            product = dot_nn(x[f], wtqkv[:, 2 * D + first : 2 * D + last]).astype(BF)
            tv[:, frame_rows, first:last] = product.reshape(PATCH, SEQ, last - first)

        @pl.when(f == 0)
        def _():
            own_caption.wait()
            landed(cap.at[pl.ds(0, SEQ - 1)], c_recv)
            for head in range(HEADS):
                first, last = window(head)
                cap_keys[head, :, : last - first] = lax.dot_general(
                    cap[head], placed(head), (((0,), (0,)), ((), ())), preferred_element_type=F32
                ).astype(BF)

        return 0

    lax.fori_loop(0, LOCAL, temporal_qkv, 0)

    frames_all = LOCAL * SEQ

    def temporal(p, _):
        for first, last in spans(0, D, 384):
            tvt[first:last, :] = tv[p, :, first:last].astype(F32).T

        def score(head):
            first, last = window(head)
            return dot_nt(tqk[p, :, D + first : D + last] * head_mask(head), tqk[p, :, first:last])

        def store(head, rows):
            tmix_t[HEAD * head : HEAD * (head + 1), :frames_all] = rows

        attend_heads(
            score, lambda head: tvt[HEAD * head : HEAD * (head + 1), :frames_all].astype(BF), store,
            (tscores, tweights, tinverse), 8,
        )
        for first, last in spans(0, D, 384):
            block = tmix_t[first:last, :].T.astype(BF)
            for f in range(LOCAL):
                tmix[f, pl.ds(pl.multiple_of(p * SEQ, SEQ), SEQ), first:last] = block[f * SEQ : (f + 1) * SEQ]

        @pl.when(p == 2)
        def _():
            last_gather()

        return 0

    tv[:, frames_all:, :] = jnp.zeros((PATCH, LANES - frames_all, D), BF)
    tmix_t[...] = jnp.zeros((D, LANES), F32)
    lax.fori_loop(0, PATCH, temporal, 0)

    load(7).wait()
    for f in range(LOCAL):
        landed(sent.at[f, pl.ds(0, SEQ - 1)], f_send.at[f])

    def finish(f, _):
        after = modulated
        for first, last in spans(0, D):
            branch = dot_nn(tmix[f], wtp[:, first:last])
            after[:, first:last] = (
                x[f, :, first:last].astype(F32) + modulation[2:3, first:last] * branch
            ).astype(BF)

        @pl.when(f == 0)
        def _():
            for half in range(2):
                landed(wg.at[core, pl.ds(0, 4)], s_recv.at[half])

        for first, last in spans(0, D):
            qk[:, first:last] = dot_nn(after[...], wg[0, :, :, first:last].reshape(D, last - first)).astype(BF)

        def score(head):
            first, last = window(head)
            return dot_nt(cap_keys[head, :, : last - first], qk[:, first:last])

        def store(head, rows):
            mix_t[HEAD * head : HEAD * (head + 1), :] = rows

        allowed = lax.broadcasted_iota(jnp.int32, (CAP, ROWS), 0) < caption_len[0]
        attend_heads(score, lambda head: cap[HEADS + head], store, (cscores, cweights, cinverse), 4, allowed)
        for first, last in spans(0, D):
            mix[:, first:last] = mix_t[first:last, :].T.astype(BF)
        order = patch_to_frame()
        for first, last in spans(0, D):
            branch = dot_nn(mix[...], wg[1, :, :, first:last].reshape(D, last - first))
            rows = (after[:, first:last].astype(F32) + branch).astype(BF)
            sent[f, :, :, first:last] = dot_nn(order, rows).reshape(SEQ, PATCH, last - first).astype(BF)

        @pl.loop(1, SEQ)
        def _(k):
            peer = peer_of(k)
            pltpu.make_async_remote_copy(
                sent.at[f, peer], out_ref.at[f, me], r_send.at[f], r_recv.at[f],
                device_id={"seq": peer}, device_id_type=MESH,
            ).start()

        pltpu.make_async_copy(sent.at[f, me], out_ref.at[f, me], local_sem.at[2 + f]).start()
        return 0

    lax.fori_loop(0, LOCAL, finish, 0)

    for f in range(LOCAL):
        pltpu.make_async_copy(sent.at[f, me], out_ref.at[f, me], local_sem.at[2 + f]).wait()
        landed(sent.at[f, pl.ds(0, SEQ - 1)], r_send.at[f])
        landed(out_ref.at[f, pl.ds(0, SEQ - 1)], r_recv.at[f])
    landed(wy.at[pl.ds(0, 3)], y_send)
    landed(wy.at[pl.ds(0, 12)], g_send)
    landed(wg.at[core, pl.ds(0, 4)], z_send)
    for half in range(2):
        landed(wg.at[core, pl.ds(0, 4)], s_send.at[half])
    landed(cap.at[pl.ds(0, SEQ - 1)], c_send)


def shards(
    frames_in, modulation, caption_kv, caption_len,
    w_spatial_qkv, w_spatial_proj, w_temporal_qkv, w_temporal_proj, w_cross_q, w_cross_out,
):
    vmem = pl.BlockSpec(memory_space=pltpu.VMEM)
    whole = pl.BlockSpec(memory_space=pl.ANY)
    dma = pltpu.SemaphoreType.DMA
    out = pl.pallas_call(
        kernel,
        out_shape=jax.ShapeDtypeStruct((LOCAL, SEQ, PATCH, D), BF),
        in_specs=[pl.BlockSpec(memory_space=pltpu.SMEM), whole, vmem] + [whole] * 7,
        out_specs=whole,
        scratch_shapes=[
            pltpu.VMEM((LOCAL, ROWS, D), BF),
            pltpu.VMEM((D, 3 * D), BF),
            pltpu.VMEM((D, D), BF),
            pltpu.VMEM((D, 3 * D), BF),
            pltpu.VMEM((D, D), BF),
            pltpu.VMEM((16, 36, D), BF),
            pltpu.VMEM((2, 8, 144, D), BF),
            pltpu.VMEM((SEQ, HEAD, CAP), BF),
            pltpu.VMEM((HEADS, CAP, 2 * LANES), BF),
            pltpu.VMEM((ROWS, D), BF),
            pltpu.VMEM((ROWS, 2 * D), BF),
            pltpu.VMEM((D, ROWS), F32),
            pltpu.VMEM((D, ROWS), F32),
            pltpu.VMEM((ROWS, D), BF),
            pltpu.VMEM((LOCAL, SEQ, PATCH, D), BF),
            pltpu.VMEM((LOCAL, SEQ, PATCH, D), BF),
            pltpu.VMEM((LOCAL, ROWS, D), BF),
            pltpu.VMEM((PATCH, LOCAL * SEQ, 2 * D), BF),
            pltpu.VMEM((PATCH, LANES, D), BF),
            pltpu.VMEM((D, LANES), F32),
            pltpu.VMEM((D, LANES), F32),
            pltpu.VMEM((LOCAL, ROWS, D), BF),
            pltpu.VMEM((2, 4, ROWS, ROWS), F32),
            pltpu.VMEM((2, 4, ROWS, ROWS), BF),
            pltpu.VMEM((2, 4, 1, ROWS), F32),
            pltpu.VMEM((2, 8, LOCAL * SEQ, LOCAL * SEQ), F32),
            pltpu.VMEM((2, 8, LOCAL * SEQ, LOCAL * SEQ), BF),
            pltpu.VMEM((2, 8, 1, LOCAL * SEQ), F32),
            pltpu.VMEM((2, 4, CAP, ROWS), F32),
            pltpu.VMEM((2, 4, CAP, ROWS), BF),
            pltpu.VMEM((2, 4, 1, ROWS), F32),
            dma((8,)),
            dma, dma, dma, dma, dma, dma, dma((2,)), dma((2,)), dma, dma,
            dma((LOCAL,)), dma((LOCAL,)), dma((LOCAL,)), dma((LOCAL,)),
            dma((5,)),
        ],
        compiler_params=pltpu.CompilerParams(
            collective_id=0, has_side_effects=True, vmem_limit_bytes=64 * 1024 * 1024
        ),
        name="block",
    )(
        caption_len, frames_in, modulation, caption_kv.T,
        w_spatial_qkv, w_spatial_proj, w_temporal_qkv, w_temporal_proj, w_cross_q, w_cross_out,
    )
    return out.reshape(frames_in.shape)


def solution(mesh):
    in_specs = (
        P(("dp", "seq"), None, None),
        P("dp", None),
        P("dp", "seq"),
        P("dp"),
        P(),
        P(),
        P(),
        P(),
        P("seq", None),
        P("seq", None),
    )
    out_specs = P(("dp", "seq"), None, None)
    return jax.shard_map(shards, mesh=mesh, in_specs=in_specs, out_specs=out_specs, check_vma=False)
```

time: 150 us -> 101 us (0.67)
  Pallas kernels: 144 us -> 96.5 us
  other arithmetic: 1.63 us -> 0 us
    pallas_call x1, Pallas kernels: 144 us -> 96.5 us  [shards(): pl.pallas_call(kernel, out_shape=jax.ShapeDtypeStruct((LOCAL, SEQ, PATCH,...]
    another operation x1 -> x0, other arithmetic: 1.63 us -> none  [shards(): crossed = jnp.stack([w_cross_q, w_cross_out])]
    unnamed x2 -> x1, local copies, waits for them, and re-layouts: 3.64 us -> 2.82 us
where the time goes in v2:
time: 101 us; the launch traced here: 100 us
  Pallas kernels  96.5 us (96%)
  local copies, waits for them, and re-layouts  2.82 us (3%)
    pallas_call x1, Pallas kernels, shards(): pl.pallas_call(kernel, out_shape=jax.ShapeDtypeStruct((LOCAL, SEQ, PATCH,...  96.5 us
    unnamed x1, local copies, waits for them, and re-layouts  2.82 us

profile of v2, /device:TPU:0, one launch (start us, length us, event | category | flops | bytes accessed | tf_op | source)
XLA Modules:
  0.0 100.0 jit_solution(16425076459499347954)
XLA Ops:
  0.7 96.5 %block.1 = bf16[3,32,8,1152]{3,2,1,0:T(8,128)(2,1)} custom-call(s32[1]{0:T(128)S(6)} %copy.12.caption_len, bf16[3,256,1152]{2,1,0:T(8,128)(2,1)} %frames_ref.1, f32[3,1152]{1,0:T(4,128)} %modulation.1, bf16[72,120]{1,0:T(8,128)(2,1)} %bitcast.3, bf16[1152,3456]{1,0:T(8,128)(2,1)} %wsqkv_ref.1, bf16[1152,1152]{1,0:T(8,128)(2,1)} %wsp_ref.1, ...), custom_call_target="tpu_custom_call" | custom-call | tf_op jit(solution)/shard_map/block/pallas_call | solution.py:444
  97.2 2.8 %copy.13 = bf16[3,256,1152]{2,1,0:T(8,128)(2,1)} copy(bf16[3,256,1152]{2,1,0:T(8,128)(2,1)} %bitcast.2) | data formatting | bytes 3538944

commit v3 on v2

--- a/solution.py
+++ b/solution.py
@@ -16,6 +16,7 @@
 PATCH = 8
 CAP = 120
 ROWS = 256
+HALVES = ((0, 640), (640, D))
 BF = jnp.bfloat16
 F32 = jnp.float32
 MESH = pl.DeviceIdType.MESH
@@ -150,62 +151,99 @@
     own_caption = pltpu.make_async_copy(caption_ref, cap.at[me], local_sem.at[0])
     own_caption.start()
 
-    def own_weight(source):
-        return pltpu.make_async_copy(source, wy.at[my_x * 4 + my_y], local_sem.at[1])
-
-    def first_gather(source):
-        own_weight(source).start()
-
-        @pl.loop(1, 4)
-        def _(k):
-            peer = (my_x + core * k) % 4 * 8 + my_z * 4 + (my_y + (1 - core) * k) % 4
-            pltpu.make_async_remote_copy(
-                source, wy.at[my_x * 4 + my_y], y_send, y_recv, device_id={"seq": peer}, device_id_type=MESH
-            ).start()
-
-    def second_gather():
-        own_weight(wcq_ref).wait()
-        landed(wy.at[pl.ds(0, 3)], y_recv)
-
-        @pl.loop(0, 12)
-        def _(n):
-            k, i = 1 + n // 4, n % 4
-            slot = (1 - core) * (my_x * 4 + i) + core * (i * 4 + my_y)
-            peer = (my_x + (1 - core) * k) % 4 * 8 + my_z * 4 + (my_y + core * k) % 4
-            pltpu.make_async_remote_copy(
-                wy.at[slot], wy.at[slot], g_send, g_recv, device_id={"seq": peer}, device_id_type=MESH
-            ).start()
-
-    def third_gather():
-        landed(wy.at[pl.ds(0, 12)], g_recv)
-        for group in range(4):
-            for first, last in spans(0, D):
+    def by_core(step):
+        for c in range(2):
+            @pl.when(core == c)
+            def _():
+                step(c, slice(*HALVES[c]))
+
+    def own_weight(m, columns):
+        source = (wcq_ref, wco_ref)[m].at[:, columns]
+        return pltpu.make_async_copy(source, wy.at[m, my_x * 4 + my_y, :, columns], local_sem.at[5 + m])
+
+    def first_gather(c, columns):
+        for m in range(2):
+            own_weight(m, columns).start()
+
+        for m, source in enumerate((wcq_ref, wco_ref)):
+            @pl.loop(1, 4)
+            def _(k):
+                peer = (my_x + c * k) % 4 * 8 + my_z * 4 + (my_y + (1 - c) * k) % 4
+                pltpu.make_async_remote_copy(
+                    source.at[:, columns], wy.at[m, my_x * 4 + my_y, :, columns], y_send.at[m], y_recv.at[m],
+                    device_id={"seq": peer}, device_id_type=MESH,
+                ).start()
+
+    def second_gather(m):
+        def step(c, columns):
+            own_weight(m, columns).wait()
+            landed(wy.at[m, pl.ds(0, 3), :, columns], y_recv.at[m])
+
+            @pl.loop(0, 12)
+            def _(n):
+                k, i = 1 + n // 4, n % 4
+                block = wy.at[m, my_x * 4 + i if c == 0 else i * 4 + my_y, :, columns]
+                peer = (my_x + (1 - c) * k) % 4 * 8 + my_z * 4 + (my_y + c * k) % 4
+                pltpu.make_async_remote_copy(
+                    block, block, g_send.at[m], g_recv.at[m], device_id={"seq": peer}, device_id_type=MESH
+                ).start()
+
+        by_core(step)
+
+    def swap(m, block, half, columns):
+        part = wg.at[m, block, :, columns]
+        return pltpu.make_async_remote_copy(
+            part, part, s_send.at[m, half], s_recv.at[m, half], device_id={"dp": other_core}, device_id_type=MESH
+        )
+
+    def third_gather(m):
+        def step(c, columns):
+            landed(wy.at[m, pl.ds(0, 12), :, columns], g_recv.at[m])
+            for group in range(4):
                 total = None
                 for y in range(4):
                     row = lax.broadcasted_iota(jnp.int32, (144, 36), 0)
                     column = lax.broadcasted_iota(jnp.int32, (144, 36), 1)
                     place = jnp.where(row == column + 36 * y, 1.0, 0.0).astype(BF)
-                    term = dot_nn(place, wy[group * 4 + y, :, first:last])
+                    term = dot_nn(place, wy[m, group * 4 + y, :, columns])
                     total = term if total is None else total + term
-                wg[core, group * 2 + my_z, :, first:last] = total.astype(BF)
-        for group in range(4):
-            block = wg.at[core, group * 2 + my_z]
-            pltpu.make_async_remote_copy(
-                block, block, z_send, z_recv,
-                device_id={"dp": dp if group == 0 else across, "seq": facing}, device_id_type=MESH,
-            ).start()
-            swap(group * 2 + my_z, 0).start()
-
-    def swap(block, half):
-        return pltpu.make_async_remote_copy(
-            wg.at[core, block], wg.at[core, block], s_send.at[half], s_recv.at[half],
-            device_id={"dp": other_core}, device_id_type=MESH,
-        )
-
-    def last_gather():
-        landed(wg.at[core, pl.ds(0, 4)], z_recv)
-        for group in range(4):
-            swap(group * 2 + 1 - my_z, 1).start()
+                wg[m, group * 2 + my_z, :, columns] = total.astype(BF)
+            for group in range(4):
+                block = wg.at[m, group * 2 + my_z, :, columns]
+                pltpu.make_async_remote_copy(
+                    block, block, z_send.at[m], z_recv.at[m],
+                    device_id={"dp": dp if group < 2 * m else across, "seq": facing}, device_id_type=MESH,
+                ).start()
+                swap(m, group * 2 + my_z, 0, columns).start()
+
+        by_core(step)
+
+    def last_gather(m):
+        def step(c, columns):
+            landed(wg.at[m, pl.ds(0, 4), :, columns], z_recv.at[m])
+            for group in range(4):
+                swap(m, group * 2 + 1 - my_z, 1, columns).start()
+
+        by_core(step)
+
+    def whole_weight(m):
+        def step(c, columns):
+            for half in range(2):
+                landed(wg.at[m, pl.ds(0, 4), :, slice(*HALVES[1 - c])], s_recv.at[m, half])
+
+        by_core(step)
+
+    def sent_weights(c, columns):
+        for m in range(2):
+            landed(wy.at[m, pl.ds(0, 3), :, columns], y_send.at[m])
+            landed(wy.at[m, pl.ds(0, 12), :, columns], g_send.at[m])
+            landed(wg.at[m, pl.ds(0, 4), :, columns], z_send.at[m])
+            for half in range(2):
+                landed(wg.at[m, pl.ds(0, 4), :, columns], s_send.at[m, half])
+
+    pl.semaphore_wait(barrier, SEQ + 1)
+
+    by_core(first_gather)
 
     def spatial(f, _):
         @pl.when(f == 0)
@@ -227,16 +265,6 @@
 
         @pl.when(f == 0)
         def _():
-            pl.semaphore_wait(barrier, SEQ + 1)
-
-            @pl.when(core == 0)
-            def _():
-                first_gather(wcq_ref)
-
-            @pl.when(core == 1)
-            def _():
-                first_gather(wco_ref)
-
             load(1).wait()
             load(3).start()
             load(4).start()
@@ -248,6 +276,7 @@
         def _():
             load(2).wait()
             load(5).start()
+            second_gather(0)
 
         for first, last in spans(1024, 2 * D):
             qk[:, first:last] = dot_nn(modulated[...], wsqkv[:, first:last]).astype(BF)
@@ -256,20 +285,9 @@
         def _():
             load(3).wait()
             load(6).start()
-            second_gather()
-
-            @pl.loop(1, SEQ)
-            def _(k):
-                pltpu.make_async_remote_copy(
-                    caption_ref, cap.at[me], c_send, c_recv, device_id={"seq": peer_of(k)}, device_id_type=MESH
-                ).start()
 
         for first, last in spans(0, D):
             vt[first:last, :] = dot_nn(modulated[...], wsqkv[:, 2 * D + first : 2 * D + last]).T
-
-        @pl.when(f == 1)
-        def _():
-            third_gather()
 
         def score(head):
             first, last = window(head)
@@ -283,6 +301,10 @@
         )
         for first, last in spans(0, D):
             mix[:, first:last] = mix_t[first:last, :].T.astype(BF)
+
+        @pl.when(f == 1)
+        def _():
+            third_gather(0)
 
         @pl.when(f == 0)
         def _():
@@ -306,6 +328,13 @@
         return 0
 
     lax.fori_loop(0, LOCAL, spatial, 0)
+    second_gather(1)
+
+    @pl.loop(1, SEQ)
+    def _(k):
+        pltpu.make_async_remote_copy(
+            caption_ref, cap.at[me], c_send, c_recv, device_id={"seq": peer_of(k)}, device_id_type=MESH
+        ).start()
 
     def temporal_qkv(f, _):
         landed(received.at[f, pl.ds(0, SEQ - 1)], f_recv.at[f])
@@ -326,19 +355,10 @@
             product = dot_nn(x[f], wtqkv[:, 2 * D + first : 2 * D + last]).astype(BF)
             tv[:, frame_rows, first:last] = product.reshape(PATCH, SEQ, last - first)
 
-        @pl.when(f == 0)
-        def _():
-            own_caption.wait()
-            landed(cap.at[pl.ds(0, SEQ - 1)], c_recv)
-            for head in range(HEADS):
-                first, last = window(head)
-                cap_keys[head, :, : last - first] = lax.dot_general(
-                    cap[head], placed(head), (((0,), (0,)), ((), ())), preferred_element_type=F32
-                ).astype(BF)
-
         return 0
 
     lax.fori_loop(0, LOCAL, temporal_qkv, 0)
+    last_gather(0)
 
     frames_all = LOCAL * SEQ
 
@@ -362,9 +382,19 @@
             for f in range(LOCAL):
                 tmix[f, pl.ds(pl.multiple_of(p * SEQ, SEQ), SEQ), first:last] = block[f * SEQ : (f + 1) * SEQ]
 
-        @pl.when(p == 2)
-        def _():
-            last_gather()
+        @pl.when(p == 4)
+        def _():
+            own_caption.wait()
+            landed(cap.at[pl.ds(0, SEQ - 1)], c_recv)
+            for head in range(HEADS):
+                first, last = window(head)
+                cap_keys[head, :, : last - first] = lax.dot_general(
+                    cap[head], placed(head), (((0,), (0,)), ((), ())), preferred_element_type=F32
+                ).astype(BF)
+
+        @pl.when(p == 5)
+        def _():
+            third_gather(1)
 
         return 0
 
@@ -386,8 +416,8 @@
 
         @pl.when(f == 0)
         def _():
-            for half in range(2):
-                landed(wg.at[core, pl.ds(0, 4)], s_recv.at[half])
+            whole_weight(0)
+            last_gather(1)
 
         for first, last in spans(0, D):
             qk[:, first:last] = dot_nn(after[...], wg[0, :, :, first:last].reshape(D, last - first)).astype(BF)
@@ -403,6 +433,11 @@
         attend_heads(score, lambda head: cap[HEADS + head], store, (cscores, cweights, cinverse), 4, allowed)
         for first, last in spans(0, D):
             mix[:, first:last] = mix_t[first:last, :].T.astype(BF)
+
+        @pl.when(f == 0)
+        def _():
+            whole_weight(1)
+
         order = patch_to_frame()
         for first, last in spans(0, D):
             branch = dot_nn(mix[...], wg[1, :, :, first:last].reshape(D, last - first))
@@ -426,11 +461,7 @@
         pltpu.make_async_copy(sent.at[f, me], out_ref.at[f, me], local_sem.at[2 + f]).wait()
         landed(sent.at[f, pl.ds(0, SEQ - 1)], r_send.at[f])
         landed(out_ref.at[f, pl.ds(0, SEQ - 1)], r_recv.at[f])
-    landed(wy.at[pl.ds(0, 3)], y_send)
-    landed(wy.at[pl.ds(0, 12)], g_send)
-    landed(wg.at[core, pl.ds(0, 4)], z_send)
-    for half in range(2):
-        landed(wg.at[core, pl.ds(0, 4)], s_send.at[half])
+    by_core(sent_weights)
     landed(cap.at[pl.ds(0, SEQ - 1)], c_send)
 
 
@@ -452,7 +483,7 @@
             pltpu.VMEM((D, D), BF),
             pltpu.VMEM((D, 3 * D), BF),
             pltpu.VMEM((D, D), BF),
-            pltpu.VMEM((16, 36, D), BF),
+            pltpu.VMEM((2, 16, 36, D), BF),
             pltpu.VMEM((2, 8, 144, D), BF),
             pltpu.VMEM((SEQ, HEAD, CAP), BF),
             pltpu.VMEM((HEADS, CAP, 2 * LANES), BF),
@@ -479,9 +510,9 @@
             pltpu.VMEM((2, 4, CAP, ROWS), BF),
             pltpu.VMEM((2, 4, 1, ROWS), F32),
             dma((8,)),
-            dma, dma, dma, dma, dma, dma, dma((2,)), dma((2,)), dma, dma,
+            dma((2,)), dma((2,)), dma((2,)), dma((2,)), dma((2,)), dma((2,)), dma((2, 2)), dma((2, 2)), dma, dma,
             dma((LOCAL,)), dma((LOCAL,)), dma((LOCAL,)), dma((LOCAL,)),
-            dma((5,)),
+            dma((7,)),
         ],
         compiler_params=pltpu.CompilerParams(
             collective_id=0, has_side_effects=True, vmem_limit_bytes=64 * 1024 * 1024

time: 101 us -> 95 us (0.941)
  Pallas kernels: 96.5 us -> 90.9 us
    pallas_call x1, Pallas kernels: 96.5 us -> 90.9 us  [shards(): pl.pallas_call(kernel, out_shape=jax.ShapeDtypeStruct((LOCAL, SEQ, PATCH,...]
where the time goes in v3:
time: 95 us; the launch traced here: 94.3 us
  Pallas kernels  90.9 us (96%)
  local copies, waits for them, and re-layouts  2.82 us (3%)
    pallas_call x1, Pallas kernels, shards(): pl.pallas_call(kernel, out_shape=jax.ShapeDtypeStruct((LOCAL, SEQ, PATCH,...  90.9 us
    unnamed x1, local copies, waits for them, and re-layouts  2.82 us

profile of v3, /device:TPU:0, one launch (start us, length us, event | category | flops | bytes accessed | tf_op | source)
XLA Modules:
  0.0 94.3 jit_solution(14288734088608270512)
XLA Ops:
  0.7 90.9 %block.1 = bf16[3,32,8,1152]{3,2,1,0:T(8,128)(2,1)} custom-call(s32[1]{0:T(128)S(6)} %copy.12.caption_len, bf16[3,256,1152]{2,1,0:T(8,128)(2,1)} %frames_ref.1, f32[3,1152]{1,0:T(4,128)} %modulation.1, bf16[72,120]{1,0:T(8,128)(2,1)} %bitcast.3, bf16[1152,3456]{1,0:T(8,128)(2,1)} %wsqkv_ref.1, bf16[1152,1152]{1,0:T(8,128)(2,1)} %wsp_ref.1, ...), custom_call_target="tpu_custom_call" | custom-call | tf_op jit(solution)/shard_map/block/pallas_call | solution.py:475
  91.5 2.8 %copy.13 = bf16[3,256,1152]{2,1,0:T(8,128)(2,1)} copy(bf16[3,256,1152]{2,1,0:T(8,128)(2,1)} %bitcast.2) | data formatting | bytes 3538944

commit v4 on v3

--- a/solution.py
+++ b/solution.py
@@ -174,15 +174,32 @@
                     device_id={"seq": peer}, device_id_type=MESH,
                 ).start()
 
+    def group_slot(c, i):
+        return my_x * 4 + i if c == 0 else i * 4 + my_y
+
+    def face_gather(c, columns):
+        own_weight(1, columns).wait()
+        landed(wy.at[1, pl.ds(0, 3), :, columns], y_recv.at[1])
+
+        @pl.loop(0, 4)
+        def _(i):
+            pltpu.make_async_remote_copy(
+                wy.at[1, group_slot(c, i), :, columns], wy.at[2, group_slot(c, i), :, columns],
+                z_send.at[1], z_recv.at[1], device_id={"dp": across, "seq": facing}, device_id_type=MESH,
+            ).start()
+
     def second_gather(m):
         def step(c, columns):
-            own_weight(m, columns).wait()
-            landed(wy.at[m, pl.ds(0, 3), :, columns], y_recv.at[m])
-
-            @pl.loop(0, 12)
+            if m == 0:
+                own_weight(0, columns).wait()
+                landed(wy.at[0, pl.ds(0, 3), :, columns], y_recv.at[0])
+            else:
+                landed(wy.at[2, pl.ds(0, 4), :, columns], z_recv.at[1])
+
+            @pl.loop(0, 12 * (m + 1))
             def _(n):
-                k, i = 1 + n // 4, n % 4
-                block = wy.at[m, my_x * 4 + i if c == 0 else i * 4 + my_y, :, columns]
+                k, i = 1 + n // 4 % 3, n % 4
+                block = wy.at[m + n // 12, group_slot(c, i), :, columns]
                 peer = (my_x + (1 - c) * k) % 4 * 8 + my_z * 4 + (my_y + c * k) % 4
                 pltpu.make_async_remote_copy(
                     block, block, g_send.at[m], g_recv.at[m], device_id={"seq": peer}, device_id_type=MESH
@@ -198,33 +215,29 @@
 
     def third_gather(m):
         def step(c, columns):
-            landed(wy.at[m, pl.ds(0, 12), :, columns], g_recv.at[m])
+            landed(wy.at[pl.ds(m, m + 1), pl.ds(0, 12), :, columns], g_recv.at[m])
+            for plane in range(m, 2 * m + 1):
+                for group in range(4):
+                    block = group * 2 + (my_z if plane == m else 1 - my_z)
+                    for y in range(4):
+                        wg[m, block, 36 * y : 36 * (y + 1), columns] = wy[plane, group * 4 + y, :, columns]
             for group in range(4):
-                total = None
-                for y in range(4):
-                    row = lax.broadcasted_iota(jnp.int32, (144, 36), 0)
-                    column = lax.broadcasted_iota(jnp.int32, (144, 36), 1)
-                    place = jnp.where(row == column + 36 * y, 1.0, 0.0).astype(BF)
-                    term = dot_nn(place, wy[m, group * 4 + y, :, columns])
-                    total = term if total is None else total + term
-                wg[m, group * 2 + my_z, :, columns] = total.astype(BF)
-            for group in range(4):
-                block = wg.at[m, group * 2 + my_z, :, columns]
-                pltpu.make_async_remote_copy(
-                    block, block, z_send.at[m], z_recv.at[m],
-                    device_id={"dp": dp if group < 2 * m else across, "seq": facing}, device_id_type=MESH,
-                ).start()
+                if m == 0:
+                    block = wg.at[0, group * 2 + my_z, :, columns]
+                    pltpu.make_async_remote_copy(
+                        block, block, z_send.at[0], z_recv.at[0],
+                        device_id={"dp": across, "seq": facing}, device_id_type=MESH,
+                    ).start()
+                else:
+                    swap(1, group * 2 + 1 - my_z, 1, columns).start()
                 swap(m, group * 2 + my_z, 0, columns).start()
 
         by_core(step)
 
-    def last_gather(m):
-        def step(c, columns):
-            landed(wg.at[m, pl.ds(0, 4), :, columns], z_recv.at[m])
-            for group in range(4):
-                swap(m, group * 2 + 1 - my_z, 1, columns).start()
-
-        by_core(step)
+    def last_gather(c, columns):
+        landed(wg.at[0, pl.ds(0, 4), :, columns], z_recv.at[0])
+        for group in range(4):
+            swap(0, group * 2 + 1 - my_z, 1, columns).start()
 
     def whole_weight(m):
         def step(c, columns):
@@ -234,10 +247,11 @@
         by_core(step)
 
     def sent_weights(c, columns):
+        landed(wg.at[0, pl.ds(0, 4), :, columns], z_send.at[0])
+        landed(wy.at[2, pl.ds(0, 4), :, columns], z_send.at[1])
         for m in range(2):
             landed(wy.at[m, pl.ds(0, 3), :, columns], y_send.at[m])
-            landed(wy.at[m, pl.ds(0, 12), :, columns], g_send.at[m])
-            landed(wg.at[m, pl.ds(0, 4), :, columns], z_send.at[m])
+            landed(wy.at[pl.ds(m, m + 1), pl.ds(0, 12), :, columns], g_send.at[m])
             for half in range(2):
                 landed(wg.at[m, pl.ds(0, 4), :, columns], s_send.at[m, half])
 
@@ -277,6 +291,7 @@
             load(2).wait()
             load(5).start()
             second_gather(0)
+            by_core(face_gather)
 
         for first, last in spans(1024, 2 * D):
             qk[:, first:last] = dot_nn(modulated[...], wsqkv[:, first:last]).astype(BF)
@@ -358,7 +373,7 @@
         return 0
 
     lax.fori_loop(0, LOCAL, temporal_qkv, 0)
-    last_gather(0)
+    by_core(last_gather)
 
     frames_all = LOCAL * SEQ
 
@@ -382,7 +397,36 @@
             for f in range(LOCAL):
                 tmix[f, pl.ds(pl.multiple_of(p * SEQ, SEQ), SEQ), first:last] = block[f * SEQ : (f + 1) * SEQ]
 
-        @pl.when(p == 4)
+        @pl.when(p == 6)
+        def _():
+            third_gather(1)
+
+        return 0
+
+    tv[:, frames_all:, :] = jnp.zeros((PATCH, LANES - frames_all, D), BF)
+    tmix_t[...] = jnp.zeros((D, LANES), F32)
+    lax.fori_loop(0, PATCH, temporal, 0)
+
+    load(7).wait()
+    for f in range(LOCAL):
+        landed(sent.at[f, pl.ds(0, SEQ - 1)], f_send.at[f])
+
+    def finish(f, _):
+        after = modulated
+        for first, last in spans(0, D):
+            branch = dot_nn(tmix[f], wtp[:, first:last])
+            after[:, first:last] = (
+                x[f, :, first:last].astype(F32) + modulation[2:3, first:last] * branch
+            ).astype(BF)
+
+        @pl.when(f == 0)
+        def _():
+            whole_weight(0)
+
+        for first, last in spans(0, D):
+            qk[:, first:last] = dot_nn(after[...], wg[0, :, :, first:last].reshape(D, last - first)).astype(BF)
+
+        @pl.when(f == 0)
         def _():
             own_caption.wait()
             landed(cap.at[pl.ds(0, SEQ - 1)], c_recv)
@@ -391,36 +435,6 @@
                 cap_keys[head, :, : last - first] = lax.dot_general(
                     cap[head], placed(head), (((0,), (0,)), ((), ())), preferred_element_type=F32
                 ).astype(BF)
-
-        @pl.when(p == 5)
-        def _():
-            third_gather(1)
-
-        return 0
-
-    tv[:, frames_all:, :] = jnp.zeros((PATCH, LANES - frames_all, D), BF)
-    tmix_t[...] = jnp.zeros((D, LANES), F32)
-    lax.fori_loop(0, PATCH, temporal, 0)
-
-    load(7).wait()
-    for f in range(LOCAL):
-        landed(sent.at[f, pl.ds(0, SEQ - 1)], f_send.at[f])
-
-    def finish(f, _):
-        after = modulated
-        for first, last in spans(0, D):
-            branch = dot_nn(tmix[f], wtp[:, first:last])
-            after[:, first:last] = (
-                x[f, :, first:last].astype(F32) + modulation[2:3, first:last] * branch
-            ).astype(BF)
-
-        @pl.when(f == 0)
-        def _():
-            whole_weight(0)
-            last_gather(1)
-
-        for first, last in spans(0, D):
-            qk[:, first:last] = dot_nn(after[...], wg[0, :, :, first:last].reshape(D, last - first)).astype(BF)
 
         def score(head):
             first, last = window(head)
@@ -474,7 +488,7 @@
     dma = pltpu.SemaphoreType.DMA
     out = pl.pallas_call(
         kernel,
-        out_shape=jax.ShapeDtypeStruct((LOCAL, SEQ, PATCH, D), BF),
+        out_shape=pltpu.VMEM((LOCAL, SEQ, PATCH, D), BF),
         in_specs=[pl.BlockSpec(memory_space=pltpu.SMEM), whole, vmem] + [whole] * 7,
         out_specs=whole,
         scratch_shapes=[
@@ -483,7 +497,7 @@
             pltpu.VMEM((D, D), BF),
             pltpu.VMEM((D, 3 * D), BF),
             pltpu.VMEM((D, D), BF),
-            pltpu.VMEM((2, 16, 36, D), BF),
+            pltpu.VMEM((3, 16, 36, D), BF),
             pltpu.VMEM((2, 8, 144, D), BF),
             pltpu.VMEM((SEQ, HEAD, CAP), BF),
             pltpu.VMEM((HEADS, CAP, 2 * LANES), BF),
@@ -515,7 +529,7 @@
             dma((7,)),
         ],
         compiler_params=pltpu.CompilerParams(
-            collective_id=0, has_side_effects=True, vmem_limit_bytes=64 * 1024 * 1024
+            collective_id=0, has_side_effects=True, vmem_limit_bytes=60 * 1024 * 1024
         ),
         name="block",
     )(

time: 95 us -> 85.5 us (0.900)
  Pallas kernels: 90.9 us -> 83.4 us
  local copies, waits for them, and re-layouts: 2.82 us -> 1.21 us
    pallas_call x1, Pallas kernels: 90.9 us -> 83.4 us  [shards(): pl.pallas_call(kernel, out_shape=pltpu.VMEM((LOCAL, SEQ, PATCH, D), BF),...]
    unnamed x1, local copies, waits for them, and re-layouts: 2.82 us -> 1.21 us
where the time goes in v4:
time: 85.5 us; the launch traced here: 85.3 us
  Pallas kernels  83.4 us (98%)
  local copies, waits for them, and re-layouts  1.21 us (1%)
    pallas_call x1, Pallas kernels, shards(): pl.pallas_call(kernel, out_shape=pltpu.VMEM((LOCAL, SEQ, PATCH, D), BF),...  83.4 us

profile of v4, /device:TPU:0, one launch (start us, length us, event | category | flops | bytes accessed | tf_op | source)
XLA Modules:
  0.0 85.3 jit_solution(12561487989976373202)
XLA Ops:
  0.7 83.4 %block.1 = bf16[3,32,8,1152]{3,2,1,0:T(8,128)(2,1)S(1)} custom-call(s32[1]{0:T(128)S(6)} %copy.13.caption_len, bf16[3,256,1152]{2,1,0:T(8,128)(2,1)} %frames_ref.1, f32[3,1152]{1,0:T(4,128)} %modulation.1, bf16[72,120]{1,0:T(8,128)(2,1)} %bitcast.3, bf16[1152,3456]{1,0:T(8,128)(2,1)} %wsqkv_ref.1, bf16[1152,1152]{1,0:T(8,128)(2,1)} %wsp_ref.1, ...), custom_call_target="tpu_custom_call" | custom-call | tf_op jit(solution)/shard_map/block/pallas_call | solution.py:489
  84.1 1.2 %copy.12 = bf16[3,256,1152]{2,1,0:T(8,128)(2,1)} copy(bf16[3,256,1152]{2,1,0:T(8,128)(2,1)S(1)} %bitcast.2) | data formatting | bytes 3538944

commit v5 on v4

--- a/solution.py
+++ b/solution.py
@@ -16,6 +16,7 @@
 PATCH = 8
 CAP = 120
 ROWS = 256
+HALF = 128
 HALVES = ((0, 640), (640, D))
 BF = jnp.bfloat16
 F32 = jnp.float32
@@ -51,15 +52,15 @@
 
 
 def frame_to_patch():
-    row = lax.broadcasted_iota(jnp.int32, (ROWS, ROWS), 0)
-    column = lax.broadcasted_iota(jnp.int32, (ROWS, ROWS), 1)
-    return jnp.where(column == (row % SEQ) * PATCH + row // SEQ, 1.0, 0.0).astype(BF)
+    row = lax.broadcasted_iota(jnp.int32, (HALF, HALF), 0)
+    column = lax.broadcasted_iota(jnp.int32, (HALF, HALF), 1)
+    return jnp.where(column == (row % 16) * PATCH + row // 16, 1.0, 0.0).astype(BF)
 
 
 def patch_to_frame():
-    row = lax.broadcasted_iota(jnp.int32, (ROWS, ROWS), 0)
-    column = lax.broadcasted_iota(jnp.int32, (ROWS, ROWS), 1)
-    return jnp.where(column == (row % PATCH) * SEQ + row // PATCH, 1.0, 0.0).astype(BF)
+    row = lax.broadcasted_iota(jnp.int32, (HALF, HALF), 0)
+    column = lax.broadcasted_iota(jnp.int32, (HALF, HALF), 1)
+    return jnp.where(column == (row % PATCH) * 16 + row // PATCH, 1.0, 0.0).astype(BF)
 
 
 def spans(first, last, step=512):
@@ -121,6 +122,18 @@
         x_ = (my_x + (k // 4) % 4) % 4
         z = (my_z + k // 16) % 2
         return x_ * 8 + z * 4 + y
+
+    def place_of(x_, z, y):
+        return (x_ + z + y) % 2 * 16 + x_ * 4 + z * 2 + y // 2
+
+    my_place = place_of(my_x, my_z, my_y)
+    my_parity = my_place // 16
+
+    def parity_peer(turn, n):
+        k_x, k_z = n // 4, n // 2 % 2
+        k_y = n % 2 * 2 + (k_x + k_z + 1 + turn) % 2
+        x_, z, y = (my_x + k_x) % 4, (my_z + k_z) % 2, (my_y + k_y) % 4
+        return x_ * 8 + z * 4 + y, place_of(x_, z, y)
 
     facing = my_x * 8 + (1 - my_z) * 4 + my_y
 
@@ -331,15 +344,16 @@
             after = frames[f, :, first:last].astype(F32) + modulation[2:3, first:last] * branch
             sent[f, :, :, first:last] = after.reshape(SEQ, PATCH, last - first).astype(BF)
 
-        @pl.loop(1, SEQ)
-        def _(k):
-            peer = peer_of(k)
-            pltpu.make_async_remote_copy(
-                sent.at[f, peer], received.at[f, me], f_send.at[f], f_recv.at[f],
-                device_id={"seq": peer}, device_id_type=MESH,
-            ).start()
-
-        received[f, me] = sent[f, me]
+        for turn in range(2):
+            @pl.loop(turn, 16)
+            def _(n):
+                peer, _ = parity_peer(turn, n)
+                pltpu.make_async_remote_copy(
+                    sent.at[f, peer], received.at[f, my_place], f_send.at[f], f_recv.at[f, turn],
+                    device_id={"seq": peer}, device_id_type=MESH,
+                ).start()
+
+        received[f, my_place] = sent[f, me]
         return 0
 
     lax.fori_loop(0, LOCAL, spatial, 0)
@@ -351,28 +365,33 @@
             caption_ref, cap.at[me], c_send, c_recv, device_id={"seq": peer_of(k)}, device_id_type=MESH
         ).start()
 
-    def temporal_qkv(f, _):
-        landed(received.at[f, pl.ds(0, SEQ - 1)], f_recv.at[f])
-
-        @pl.when(f == 0)
-        def _():
-            load(6).wait()
-
-        order = frame_to_patch()
-        for first, last in spans(0, D):
-            block = received[f, :, :, first:last].astype(F32).reshape(ROWS, last - first).astype(BF)
-            x[f, :, first:last] = dot_nn(order, block).astype(BF)
-        frame_rows = pl.ds(pl.multiple_of(f * SEQ, SEQ), SEQ)
-        for first, last in spans(0, 2 * D):
-            product = dot_nn(x[f], wtqkv[:, first:last]).astype(BF)
-            tqk[:, frame_rows, first:last] = product.reshape(PATCH, SEQ, last - first)
-        for first, last in spans(0, D):
-            product = dot_nn(x[f], wtqkv[:, 2 * D + first : 2 * D + last]).astype(BF)
-            tv[:, frame_rows, first:last] = product.reshape(PATCH, SEQ, last - first)
-
-        return 0
-
-    lax.fori_loop(0, LOCAL, temporal_qkv, 0)
+    order = frame_to_patch()
+
+    @pl.loop(0, LOCAL)
+    def _(f):
+        for turn in range(2):
+            landed(received.at[f, pl.ds(0, 16 - turn)], f_recv.at[f, turn])
+
+            if turn == 0:
+                @pl.when(f == 0)
+                def _():
+                    load(6).wait()
+
+            first_place = pl.multiple_of((my_parity + 1 + turn) % 2 * 16, 16)
+            places = pl.ds(first_place, 16)
+            for first, last in spans(0, D):
+                block = received[f, places, :, first:last].astype(F32).reshape(HALF, last - first).astype(BF)
+                block = dot_nn(order, block).astype(BF)
+                modulated[:HALF, first:last] = block
+                x[f, :, places, first:last] = block.reshape(PATCH, 16, last - first)
+            frame_rows = pl.ds(pl.multiple_of(f * SEQ + first_place, 16), 16)
+            for first, last in spans(0, 2 * D):
+                product = dot_nn(modulated[:HALF, :], wtqkv[:, first:last]).astype(BF)
+                tqk[:, frame_rows, first:last] = product.reshape(PATCH, 16, last - first)
+            for first, last in spans(0, D):
+                product = dot_nn(modulated[:HALF, :], wtqkv[:, 2 * D + first : 2 * D + last]).astype(BF)
+                tv[:, frame_rows, first:last] = product.reshape(PATCH, 16, last - first)
+
     by_core(last_gather)
 
     frames_all = LOCAL * SEQ
@@ -395,38 +414,36 @@
         for first, last in spans(0, D, 384):
             block = tmix_t[first:last, :].T.astype(BF)
             for f in range(LOCAL):
-                tmix[f, pl.ds(pl.multiple_of(p * SEQ, SEQ), SEQ), first:last] = block[f * SEQ : (f + 1) * SEQ]
-
-        @pl.when(p == 6)
-        def _():
-            third_gather(1)
-
+                tmix[f, p, :, first:last] = block[f * SEQ : (f + 1) * SEQ]
         return 0
 
     tv[:, frames_all:, :] = jnp.zeros((PATCH, LANES - frames_all, D), BF)
     tmix_t[...] = jnp.zeros((D, LANES), F32)
     lax.fori_loop(0, PATCH, temporal, 0)
+    third_gather(1)
 
     load(7).wait()
     for f in range(LOCAL):
         landed(sent.at[f, pl.ds(0, SEQ - 1)], f_send.at[f])
 
-    def finish(f, _):
+    def finish(step, _):
+        f, turn = step // 2, step % 2
+        places = pl.ds(pl.multiple_of((my_parity + 1 + turn) % 2 * 16, 16), 16)
         after = modulated
         for first, last in spans(0, D):
-            branch = dot_nn(tmix[f], wtp[:, first:last])
-            after[:, first:last] = (
-                x[f, :, first:last].astype(F32) + modulation[2:3, first:last] * branch
+            branch = dot_nn(tmix[f, :, places, :].reshape(HALF, D), wtp[:, first:last])
+            after[:HALF, first:last] = (
+                x[f, :, places, first:last].reshape(HALF, last - first).astype(F32) + modulation[2:3, first:last] * branch
             ).astype(BF)
 
-        @pl.when(f == 0)
+        @pl.when(step == 0)
         def _():
             whole_weight(0)
 
         for first, last in spans(0, D):
-            qk[:, first:last] = dot_nn(after[...], wg[0, :, :, first:last].reshape(D, last - first)).astype(BF)
-
-        @pl.when(f == 0)
+            qk[:HALF, first:last] = dot_nn(after[:HALF, :], wg[0, :, :, first:last].reshape(D, last - first)).astype(BF)
+
+        @pl.when(step == 0)
         def _():
             own_caption.wait()
             landed(cap.at[pl.ds(0, SEQ - 1)], c_recv)
@@ -438,41 +455,44 @@
 
         def score(head):
             first, last = window(head)
-            return dot_nt(cap_keys[head, :, : last - first], qk[:, first:last])
+            return dot_nt(cap_keys[head, :, : last - first], qk[:HALF, first:last])
 
         def store(head, rows):
-            mix_t[HEAD * head : HEAD * (head + 1), :] = rows
-
-        allowed = lax.broadcasted_iota(jnp.int32, (CAP, ROWS), 0) < caption_len[0]
+            mix_t[HEAD * head : HEAD * (head + 1), :HALF] = rows
+
+        allowed = lax.broadcasted_iota(jnp.int32, (CAP, HALF), 0) < caption_len[0]
         attend_heads(score, lambda head: cap[HEADS + head], store, (cscores, cweights, cinverse), 4, allowed)
         for first, last in spans(0, D):
-            mix[:, first:last] = mix_t[first:last, :].T.astype(BF)
-
-        @pl.when(f == 0)
+            mix[:HALF, first:last] = mix_t[first:last, :HALF].T.astype(BF)
+
+        @pl.when(step == 0)
         def _():
             whole_weight(1)
 
         order = patch_to_frame()
         for first, last in spans(0, D):
-            branch = dot_nn(mix[...], wg[1, :, :, first:last].reshape(D, last - first))
-            rows = (after[:, first:last].astype(F32) + branch).astype(BF)
-            sent[f, :, :, first:last] = dot_nn(order, rows).reshape(SEQ, PATCH, last - first).astype(BF)
-
-        @pl.loop(1, SEQ)
-        def _(k):
-            peer = peer_of(k)
+            branch = dot_nn(mix[:HALF, :], wg[1, :, :, first:last].reshape(D, last - first))
+            rows = (after[:HALF, first:last].astype(F32) + branch).astype(BF)
+            sent[f, places, :, first:last] = dot_nn(order, rows).reshape(16, PATCH, last - first).astype(BF)
+
+        @pl.loop(turn, 16)
+        def _(n):
+            peer, place = parity_peer(turn, n)
             pltpu.make_async_remote_copy(
-                sent.at[f, peer], out_ref.at[f, me], r_send.at[f], r_recv.at[f],
+                sent.at[f, place], out_ref.at[f, me], r_send.at[f], r_recv.at[f],
                 device_id={"seq": peer}, device_id_type=MESH,
             ).start()
 
-        pltpu.make_async_copy(sent.at[f, me], out_ref.at[f, me], local_sem.at[2 + f]).start()
+        @pl.when(turn == 1)
+        def _():
+            pltpu.make_async_copy(sent.at[f, my_place], out_ref.at[f, me], local_sem.at[2 + f]).start()
+
         return 0
 
-    lax.fori_loop(0, LOCAL, finish, 0)
+    lax.fori_loop(0, 2 * LOCAL, finish, 0)
 
     for f in range(LOCAL):
-        pltpu.make_async_copy(sent.at[f, me], out_ref.at[f, me], local_sem.at[2 + f]).wait()
+        pltpu.make_async_copy(sent.at[f, my_place], out_ref.at[f, me], local_sem.at[2 + f]).wait()
         landed(sent.at[f, pl.ds(0, SEQ - 1)], r_send.at[f])
         landed(out_ref.at[f, pl.ds(0, SEQ - 1)], r_recv.at[f])
     by_core(sent_weights)
@@ -508,24 +528,24 @@
             pltpu.VMEM((ROWS, D), BF),
             pltpu.VMEM((LOCAL, SEQ, PATCH, D), BF),
             pltpu.VMEM((LOCAL, SEQ, PATCH, D), BF),
-            pltpu.VMEM((LOCAL, ROWS, D), BF),
+            pltpu.VMEM((LOCAL, PATCH, SEQ, D), BF),
             pltpu.VMEM((PATCH, LOCAL * SEQ, 2 * D), BF),
             pltpu.VMEM((PATCH, LANES, D), BF),
             pltpu.VMEM((D, LANES), F32),
             pltpu.VMEM((D, LANES), F32),
-            pltpu.VMEM((LOCAL, ROWS, D), BF),
+            pltpu.VMEM((LOCAL, PATCH, SEQ, D), BF),
             pltpu.VMEM((2, 4, ROWS, ROWS), F32),
             pltpu.VMEM((2, 4, ROWS, ROWS), BF),
             pltpu.VMEM((2, 4, 1, ROWS), F32),
             pltpu.VMEM((2, 8, LOCAL * SEQ, LOCAL * SEQ), F32),
             pltpu.VMEM((2, 8, LOCAL * SEQ, LOCAL * SEQ), BF),
             pltpu.VMEM((2, 8, 1, LOCAL * SEQ), F32),
-            pltpu.VMEM((2, 4, CAP, ROWS), F32),
-            pltpu.VMEM((2, 4, CAP, ROWS), BF),
-            pltpu.VMEM((2, 4, 1, ROWS), F32),
+            pltpu.VMEM((2, 4, CAP, HALF), F32),
+            pltpu.VMEM((2, 4, CAP, HALF), BF),
+            pltpu.VMEM((2, 4, 1, HALF), F32),
             dma((8,)),
             dma((2,)), dma((2,)), dma((2,)), dma((2,)), dma((2,)), dma((2,)), dma((2, 2)), dma((2, 2)), dma, dma,
-            dma((LOCAL,)), dma((LOCAL,)), dma((LOCAL,)), dma((LOCAL,)),
+            dma((LOCAL,)), dma((LOCAL, 2)), dma((LOCAL,)), dma((LOCAL,)),
             dma((7,)),
         ],
         compiler_params=pltpu.CompilerParams(

time: 85.5 us -> 87.7 us (1.026)
  Pallas kernels: 83.4 us -> 85.6 us
    pallas_call x1, Pallas kernels: 83.4 us -> 85.6 us  [shards(): pl.pallas_call(kernel, out_shape=pltpu.VMEM((LOCAL, SEQ, PATCH, D), BF),...]
where the time goes in v5:
time: 87.7 us; the launch traced here: 87.5 us
  Pallas kernels  85.6 us (98%)
  local copies, waits for them, and re-layouts  1.21 us (1%)
    pallas_call x1, Pallas kernels, shards(): pl.pallas_call(kernel, out_shape=pltpu.VMEM((LOCAL, SEQ, PATCH, D), BF),...  85.6 us

profile of v5, /device:TPU:0, one launch (start us, length us, event | category | flops | bytes accessed | tf_op | source)
XLA Modules:
  0.0 87.5 jit_solution(9603905075303136364)
XLA Ops:
  0.7 85.6 %block.1 = bf16[3,32,8,1152]{3,2,1,0:T(8,128)(2,1)S(1)} custom-call(s32[1]{0:T(128)S(6)} %copy.13.caption_len, bf16[3,256,1152]{2,1,0:T(8,128)(2,1)} %frames_ref.1, f32[3,1152]{1,0:T(4,128)} %modulation.1, bf16[72,120]{1,0:T(8,128)(2,1)} %bitcast.3, bf16[1152,3456]{1,0:T(8,128)(2,1)} %wsqkv_ref.1, bf16[1152,1152]{1,0:T(8,128)(2,1)} %wsp_ref.1, ...), custom_call_target="tpu_custom_call" | custom-call | tf_op jit(solution)/shard_map/block/pallas_call | solution.py:509
  86.3 1.2 %copy.12 = bf16[3,256,1152]{2,1,0:T(8,128)(2,1)} copy(bf16[3,256,1152]{2,1,0:T(8,128)(2,1)S(1)} %bitcast.2) | data formatting | bytes 3538944

commit v6 on v5

--- a/solution.py
+++ b/solution.py
@@ -58,9 +58,9 @@
 
 
 def patch_to_frame():
-    row = lax.broadcasted_iota(jnp.int32, (HALF, HALF), 0)
-    column = lax.broadcasted_iota(jnp.int32, (HALF, HALF), 1)
-    return jnp.where(column == (row % PATCH) * 16 + row // PATCH, 1.0, 0.0).astype(BF)
+    row = lax.broadcasted_iota(jnp.int32, (ROWS, ROWS), 0)
+    column = lax.broadcasted_iota(jnp.int32, (ROWS, ROWS), 1)
+    return jnp.where(column == (row % PATCH) * SEQ + row // PATCH, 1.0, 0.0).astype(BF)
 
 
 def spans(first, last, step=512):
@@ -281,7 +281,7 @@
         def _():
             load(5).wait()
 
-        @pl.loop(0, ROWS // 32, unroll=4)
+        @pl.loop(0, ROWS // 32, unroll=8)
         def _(r):
             rows = pl.ds(pl.multiple_of(r * 32, 32), 32)
             wide = frames[f, rows, :].astype(F32)
@@ -426,24 +426,22 @@
     for f in range(LOCAL):
         landed(sent.at[f, pl.ds(0, SEQ - 1)], f_send.at[f])
 
-    def finish(step, _):
-        f, turn = step // 2, step % 2
-        places = pl.ds(pl.multiple_of((my_parity + 1 + turn) % 2 * 16, 16), 16)
+    def finish(f, _):
         after = modulated
         for first, last in spans(0, D):
-            branch = dot_nn(tmix[f, :, places, :].reshape(HALF, D), wtp[:, first:last])
-            after[:HALF, first:last] = (
-                x[f, :, places, first:last].reshape(HALF, last - first).astype(F32) + modulation[2:3, first:last] * branch
+            branch = dot_nn(tmix[f].reshape(ROWS, D), wtp[:, first:last])
+            after[:, first:last] = (
+                x[f, :, :, first:last].reshape(ROWS, last - first).astype(F32) + modulation[2:3, first:last] * branch
             ).astype(BF)
 
-        @pl.when(step == 0)
+        @pl.when(f == 0)
         def _():
             whole_weight(0)
 
         for first, last in spans(0, D):
-            qk[:HALF, first:last] = dot_nn(after[:HALF, :], wg[0, :, :, first:last].reshape(D, last - first)).astype(BF)
-
-        @pl.when(step == 0)
+            qk[:, first:last] = dot_nn(after[...], wg[0, :, :, first:last].reshape(D, last - first)).astype(BF)
+
+        @pl.when(f == 0)
         def _():
             own_caption.wait()
             landed(cap.at[pl.ds(0, SEQ - 1)], c_recv)
@@ -455,41 +453,40 @@
 
         def score(head):
             first, last = window(head)
-            return dot_nt(cap_keys[head, :, : last - first], qk[:HALF, first:last])
+            return dot_nt(cap_keys[head, :, : last - first], qk[:, first:last])
 
         def store(head, rows):
-            mix_t[HEAD * head : HEAD * (head + 1), :HALF] = rows
-
-        allowed = lax.broadcasted_iota(jnp.int32, (CAP, HALF), 0) < caption_len[0]
+            mix_t[HEAD * head : HEAD * (head + 1), :] = rows
+
+        allowed = lax.broadcasted_iota(jnp.int32, (CAP, ROWS), 0) < caption_len[0]
         attend_heads(score, lambda head: cap[HEADS + head], store, (cscores, cweights, cinverse), 4, allowed)
         for first, last in spans(0, D):
-            mix[:HALF, first:last] = mix_t[first:last, :HALF].T.astype(BF)
-
-        @pl.when(step == 0)
+            mix[:, first:last] = mix_t[first:last, :].T.astype(BF)
+
+        @pl.when(f == 0)
         def _():
             whole_weight(1)
 
         order = patch_to_frame()
         for first, last in spans(0, D):
-            branch = dot_nn(mix[:HALF, :], wg[1, :, :, first:last].reshape(D, last - first))
-            rows = (after[:HALF, first:last].astype(F32) + branch).astype(BF)
-            sent[f, places, :, first:last] = dot_nn(order, rows).reshape(16, PATCH, last - first).astype(BF)
-
-        @pl.loop(turn, 16)
-        def _(n):
-            peer, place = parity_peer(turn, n)
+            branch = dot_nn(mix[...], wg[1, :, :, first:last].reshape(D, last - first))
+            rows = (after[:, first:last].astype(F32) + branch).astype(BF)
+            sent[f, :, :, first:last] = dot_nn(order, rows).reshape(SEQ, PATCH, last - first).astype(BF)
+
+        @pl.loop(1, SEQ)
+        def _(k):
+            y = (my_y + k % 4) % 4
+            x_ = (my_x + k // 4 % 4) % 4
+            z = (my_z + k // 16) % 2
             pltpu.make_async_remote_copy(
-                sent.at[f, place], out_ref.at[f, me], r_send.at[f], r_recv.at[f],
-                device_id={"seq": peer}, device_id_type=MESH,
+                sent.at[f, place_of(x_, z, y)], out_ref.at[f, me], r_send.at[f], r_recv.at[f],
+                device_id={"seq": x_ * 8 + z * 4 + y}, device_id_type=MESH,
             ).start()
 
-        @pl.when(turn == 1)
-        def _():
-            pltpu.make_async_copy(sent.at[f, my_place], out_ref.at[f, me], local_sem.at[2 + f]).start()
-
+        pltpu.make_async_copy(sent.at[f, my_place], out_ref.at[f, me], local_sem.at[2 + f]).start()
         return 0
 
-    lax.fori_loop(0, 2 * LOCAL, finish, 0)
+    lax.fori_loop(0, LOCAL, finish, 0)
 
     for f in range(LOCAL):
         pltpu.make_async_copy(sent.at[f, my_place], out_ref.at[f, me], local_sem.at[2 + f]).wait()
@@ -540,9 +537,9 @@
             pltpu.VMEM((2, 8, LOCAL * SEQ, LOCAL * SEQ), F32),
             pltpu.VMEM((2, 8, LOCAL * SEQ, LOCAL * SEQ), BF),
             pltpu.VMEM((2, 8, 1, LOCAL * SEQ), F32),
-            pltpu.VMEM((2, 4, CAP, HALF), F32),
-            pltpu.VMEM((2, 4, CAP, HALF), BF),
-            pltpu.VMEM((2, 4, 1, HALF), F32),
+            pltpu.VMEM((2, 4, CAP, ROWS), F32),
+            pltpu.VMEM((2, 4, CAP, ROWS), BF),
+            pltpu.VMEM((2, 4, 1, ROWS), F32),
             dma((8,)),
             dma((2,)), dma((2,)), dma((2,)), dma((2,)), dma((2,)), dma((2,)), dma((2, 2)), dma((2, 2)), dma, dma,
             dma((LOCAL,)), dma((LOCAL, 2)), dma((LOCAL,)), dma((LOCAL,)),

time: 87.7 us -> 84.7 us (0.966)
  Pallas kernels: 85.6 us -> 82.7 us
    pallas_call x1, Pallas kernels: 85.6 us -> 82.7 us  [shards(): pl.pallas_call(kernel, out_shape=pltpu.VMEM((LOCAL, SEQ, PATCH, D), BF),...]
where the time goes in v6:
time: 84.7 us; the launch traced here: 84.5 us
  Pallas kernels  82.7 us (98%)
  local copies, waits for them, and re-layouts  1.21 us (1%)
    pallas_call x1, Pallas kernels, shards(): pl.pallas_call(kernel, out_shape=pltpu.VMEM((LOCAL, SEQ, PATCH, D), BF),...  82.7 us

profile of v6, /device:TPU:0, one launch (start us, length us, event | category | flops | bytes accessed | tf_op | source)
XLA Modules:
  0.0 84.5 jit_solution(15559958911789507843)
XLA Ops:
  0.7 82.7 %block.1 = bf16[3,32,8,1152]{3,2,1,0:T(8,128)(2,1)S(1)} custom-call(s32[1]{0:T(128)S(6)} %copy.13.caption_len, bf16[3,256,1152]{2,1,0:T(8,128)(2,1)} %frames_ref.1, f32[3,1152]{1,0:T(4,128)} %modulation.1, bf16[72,120]{1,0:T(8,128)(2,1)} %bitcast.3, bf16[1152,3456]{1,0:T(8,128)(2,1)} %wsqkv_ref.1, bf16[1152,1152]{1,0:T(8,128)(2,1)} %wsp_ref.1, ...), custom_call_target="tpu_custom_call" | custom-call | tf_op jit(solution)/shard_map/block/pallas_call | solution.py:506
  83.3 1.2 %copy.12 = bf16[3,256,1152]{2,1,0:T(8,128)(2,1)} copy(bf16[3,256,1152]{2,1,0:T(8,128)(2,1)S(1)} %bitcast.2) | data formatting | bytes 3538944

commit v7 on v6

--- a/solution.py
+++ b/solution.py
@@ -419,7 +419,7 @@
 
     tv[:, frames_all:, :] = jnp.zeros((PATCH, LANES - frames_all, D), BF)
     tmix_t[...] = jnp.zeros((D, LANES), F32)
-    lax.fori_loop(0, PATCH, temporal, 0)
+    lax.fori_loop(0, PATCH, temporal, 0, unroll=2)
     third_gather(1)
 
     load(7).wait()

time: 84.7 us -> 83.9 us (level)
  Pallas kernels: 82.7 us -> 81.8 us
    pallas_call x1, Pallas kernels: 82.7 us -> 81.8 us  [shards(): pl.pallas_call(kernel, out_shape=pltpu.VMEM((LOCAL, SEQ, PATCH, D), BF),...]
where the time goes in v7:
time: 83.9 us; the launch traced here: 83.7 us
  Pallas kernels  81.8 us (97%)
  local copies, waits for them, and re-layouts  1.21 us (1%)
    pallas_call x1, Pallas kernels, shards(): pl.pallas_call(kernel, out_shape=pltpu.VMEM((LOCAL, SEQ, PATCH, D), BF),...  81.8 us

profile of v7, /device:TPU:0, one launch (start us, length us, event | category | flops | bytes accessed | tf_op | source)
XLA Modules:
  0.0 83.7 jit_solution(4548823577430336429)
XLA Ops:
  0.7 81.8 %block.1 = bf16[3,32,8,1152]{3,2,1,0:T(8,128)(2,1)S(1)} custom-call(s32[1]{0:T(128)S(6)} %copy.13.caption_len, bf16[3,256,1152]{2,1,0:T(8,128)(2,1)} %frames_ref.1, f32[3,1152]{1,0:T(4,128)} %modulation.1, bf16[72,120]{1,0:T(8,128)(2,1)} %bitcast.3, bf16[1152,3456]{1,0:T(8,128)(2,1)} %wsqkv_ref.1, bf16[1152,1152]{1,0:T(8,128)(2,1)} %wsp_ref.1, ...), custom_call_target="tpu_custom_call" | custom-call | tf_op jit(solution)/shard_map/block/pallas_call | solution.py:506
  82.5 1.2 %copy.12 = bf16[3,256,1152]{2,1,0:T(8,128)(2,1)} copy(bf16[3,256,1152]{2,1,0:T(8,128)(2,1)S(1)} %bitcast.2) | data formatting | bytes 3538944
